TPU v7x, 256 devices: a whole 4x4x8 slice. The times are simulated.
256 devices in a mesh: dp: 32 (over x, z_lo, core), expert: 8 (over y, z_hi).
Axes of the slice: x: 4, y: 4, z: 8 (z_hi: 2, z_lo: 4; z = z_hi * 4 + z_lo), core: 2. Of those that a mesh axis runs over, the one named last changes fastest.
Arguments:
- queries: bfloat16 [2, 128, 4096], P(None, 'dp'), may hold values from -170 to 170
- fresh_entries: bfloat16 [2, 128, 512], P(None, 'dp'), may hold values from -6 to 6
- cache_blocks: bfloat16 [128, 32, 128, 512], P('dp', None, 'expert'), may hold values from -6 to 6
- lengths: int32 [128], P('dp'), may hold values from 256 to 4096, as said below
- migration: int32 [256, 2], P('dp'), may hold values from 0 to 31, as said below
- residual: bfloat16 [2, 128, 4096], P(None, 'dp'), may hold values from -6 to 6
- out_weight: bfloat16 [4096, 4096], P('expert'), may hold values from -1.5 to 1.5
- norm_gain: float32 [4096], replicated, may hold values from 0.1 to 1.9
- routes: int32 [2, 128, 8], P(None, 'dp'), may hold values from 0 to 63, all different within a row; in each aligned block of 4 rows (0 to 3, 4 to 7, ..., all dimensions but the last counted through in order) at most 2 rows name the same one
- route_gates: float32 [2, 128, 8], P(None, 'dp'), may hold values from 0.1 to 1
- w_gate: bfloat16 [64, 4096, 1024], P('dp', None, 'expert'), may hold values from -0.09375 to 0.09375
- w_up: bfloat16 [64, 4096, 1024], P('dp', None, 'expert'), may hold values from -0.09375 to 0.09375
- w_down: bfloat16 [64, 1024, 4096], P('dp', 'expert'), may hold values from -0.1875 to 0.1875
Outputs:
- layer_out: bfloat16 [2, 128, 4096], P(None, 'dp', 'expert')
- guest_blocks: bfloat16 [256, 128, 512], P('dp', 'expert')
Inputs may be any that keep to these rules, and one draw needn't show every extreme that they name: `lengths`: the longest request of every draw has all 4096 positions. `migration`: rows s * 8 to s * 8 + 7 name distinct pairs of a request of index s of dp (0 to 3) and a block that lies wholly below that request's length; the last block of the longest request is among them. `routes`: each row names 8 different experts; in each step the rows of one index of dp name one expert at most 2 times, a bound that some block reaches in some step and index.
All inputs are finite; a program needn't handle non-finite values.
Results may differ from a plain program's by a relative error of at most 0.027.
Values may be sent and summed in bfloat16 or wider, within the bound.
A program may use at most 320 MiB of HBM per device.

v0:
```python
import math

import jax
import jax.numpy as jnp
from jax import lax
from jax.sharding import PartitionSpec as P

D = 4096
HD = 128
QH = 32
KVH = 2
EXP_DEV = 2
TOPK = 8
BLOCKS = 32


HIGHEST = lax.Precision.HIGHEST


def combined_all(value, axis, combine):
    everything = jax.tree.map(
        lambda part, kind: lax.all_gather(part.astype(kind), axis),
        value,
        (jnp.bfloat16, jnp.bfloat16, jnp.bfloat16),
    )

    def take(k):
        return jax.tree.map(lambda part, own: part[k].astype(own.dtype), everything, value)

    return lax.fori_loop(
        1, lax.axis_size(axis), lambda k, so_far: combine(so_far, take(k)), take(0)
    )


def shifted(value, axis, steps):
    count = lax.axis_size(axis)
    pairs = [(source, (source + steps) % count) for source in range(count)]
    return lax.ppermute(value, axis, pairs)


def join_partials(left_part, right_part):
    new_peak = jnp.maximum(left_part[0], right_part[0])
    left_scale = jnp.exp(left_part[0] - new_peak)
    right_scale = jnp.exp(right_part[0] - new_peak)
    new_total = left_part[1] * left_scale + right_part[1] * right_scale
    new_weighted = left_part[2] * left_scale[..., None] + right_part[2] * right_scale[..., None]
    return (new_peak, new_total, new_weighted)


def shards(
    queries,
    fresh_entries,
    cache_blocks,
    lengths,
    migration,
    residual,
    out_weight,
    norm_gain,
    routes,
    route_gates,
    w_gate,
    w_up,
    w_down,
):
    expert_count = lax.axis_size("expert")
    expert_pos = lax.axis_index("expert")
    data_count = lax.axis_size("dp")
    local_req = cache_blocks.shape[0]
    block_rows = cache_blocks.shape[2]
    groups = QH // KVH
    own_heads = QH // expert_count
    part_width = D // expert_count
    score_scale = 1.0 / math.sqrt(HD)
    most_rows = max(2, local_req * TOPK // (EXP_DEV * data_count))
    slot_count = EXP_DEV * data_count * most_rows
    block_len = block_rows * expert_count
    positions = (
        jnp.arange(BLOCKS, dtype=jnp.int32)[:, None] * block_len
        + expert_pos * block_rows
        + jnp.arange(block_rows, dtype=jnp.int32)[None, :]
    ).reshape(-1)
    is_valid = positions[None, :] < lengths[:, None]
    stored = cache_blocks.reshape(local_req, BLOCKS * block_rows, 2, KVH, HD)
    keys_here = stored[:, :, 0]
    values_here = stored[:, :, 1]
    head_ids = expert_pos * own_heads + jnp.arange(own_heads, dtype=jnp.int32)
    head_select = (head_ids[:, None] // groups == jnp.arange(KVH, dtype=jnp.int32)[None, :]).astype(
        jnp.float32
    )
    fresh_all = fresh_entries.reshape(2, local_req, 2, KVH, HD).astype(jnp.float32)
    fresh_keys = jnp.einsum("hk,nrkd->rnhd", head_select, fresh_all[:, :, 0], precision=HIGHEST)
    fresh_values = jnp.einsum("hk,nrkd->rnhd", head_select, fresh_all[:, :, 1], precision=HIGHEST)
    picked = cache_blocks[migration[:, 0], migration[:, 1]]
    outputs = []
    guest_out = picked
    for step_idx in range(2):
        query_all = queries[step_idx].reshape(local_req, KVH, groups, HD)
        scores = (
            jnp.einsum("rkgd,rpkd->rkgp", query_all, keys_here, preferred_element_type=jnp.float32)
            * score_scale
        )
        scores = jnp.where(is_valid[:, None, None, :], scores, -jnp.inf)
        row_peak = jnp.max(scores, -1)
        weights = jnp.exp(scores - row_peak[..., None])
        row_total = jnp.sum(weights, -1).reshape(local_req, QH)
        weighted = jnp.einsum(
            "rkgp,rpkd->rkgd",
            weights.astype(jnp.bfloat16),
            values_here,
            preferred_element_type=jnp.float32,
        ).reshape(local_req, QH, HD)
        row_peak = row_peak.reshape(local_req, QH)
        peak_all, total_all, weighted_all = combined_all(
            (row_peak, row_total, weighted), "expert", join_partials
        )
        head_peak = lax.dynamic_slice_in_dim(peak_all, expert_pos * own_heads, own_heads, 1)
        head_total = lax.dynamic_slice_in_dim(total_all, expert_pos * own_heads, own_heads, 1)
        head_weighted = lax.dynamic_slice_in_dim(weighted_all, expert_pos * own_heads, own_heads, 1)
        query_own = lax.dynamic_slice_in_dim(
            queries[step_idx], expert_pos * own_heads * HD, own_heads * HD, 1
        )
        query_own = query_own.reshape(local_req, own_heads, HD).astype(jnp.float32)
        fresh_scores = (
            jnp.einsum("rhd,rnhd->rhn", query_own, fresh_keys[:, : step_idx + 1], precision=HIGHEST)
            * score_scale
        )
        new_peak = jnp.maximum(head_peak, jnp.max(fresh_scores, -1))
        rescale = jnp.exp(head_peak - new_peak)
        fresh_weights = jnp.exp(fresh_scores - new_peak[..., None])
        head_total = head_total * rescale + jnp.sum(fresh_weights, -1)
        fresh_sum = jnp.einsum(
            "rhn,rnhd->rhd",
            fresh_weights.astype(jnp.bfloat16),
            fresh_values[:, : step_idx + 1].astype(jnp.bfloat16),
            preferred_element_type=jnp.float32,
        )
        head_weighted = head_weighted * rescale[..., None] + fresh_sum
        attention = (
            (head_weighted / head_total[..., None])
            .astype(jnp.bfloat16)
            .reshape(local_req, own_heads * HD)
        )
        projected = lax.psum(
            jnp.dot(attention, out_weight, preferred_element_type=jnp.float32).astype(jnp.bfloat16),
            "expert",
        ).astype(jnp.float32)
        hidden = residual[step_idx].astype(jnp.float32) + projected
        spread = jnp.mean(hidden * hidden, -1, keepdims=True)
        normed = (hidden * lax.rsqrt(spread + 1e-06) * norm_gain).astype(jnp.bfloat16)
        flat_ids = routes[step_idx].reshape(-1)
        pair_total = flat_ids.shape[0]
        pair_order = jnp.arange(pair_total, dtype=jnp.int32)
        earlier = (flat_ids[:, None] == flat_ids[None, :]) & (
            pair_order[:, None] > pair_order[None, :]
        )
        slot_rank = jnp.sum(earlier.astype(jnp.int32), 1)
        slot_ids = flat_ids * most_rows + slot_rank
        placement_map = jnp.arange(slot_count, dtype=jnp.int32)[:, None] == slot_ids[None, :]
        token_rows = jnp.repeat(normed, TOPK, axis=0)
        outgoing = jnp.dot(
            placement_map.astype(jnp.bfloat16), token_rows, preferred_element_type=jnp.float32
        )
        outgoing = outgoing.astype(jnp.bfloat16).reshape(
            data_count, EXP_DEV, most_rows, token_rows.shape[1]
        )
        arrived = lax.all_to_all(outgoing, "dp", split_axis=0, concat_axis=0, tiled=True)
        gate_part = jnp.einsum(
            "sjmd,jdf->sjmf", arrived, w_gate, preferred_element_type=jnp.float32
        )
        up_part = jnp.einsum("sjmd,jdf->sjmf", arrived, w_up, preferred_element_type=jnp.float32)
        inner_act = (jax.nn.silu(gate_part) * up_part).astype(jnp.bfloat16)
        produced = jnp.einsum(
            "sjmf,jfd->sjmd", inner_act, w_down, preferred_element_type=jnp.float32
        )
        returned = lax.all_to_all(
            produced.astype(jnp.bfloat16), "dp", split_axis=0, concat_axis=0, tiled=True
        ).astype(produced.dtype)
        expert_out = lax.psum_scatter(
            returned.astype(jnp.bfloat16), "expert", scatter_dimension=3, tiled=True
        )
        expert_flat = expert_out.reshape(slot_count, part_width).astype(jnp.float32)
        gate_map = placement_map.astype(jnp.float32) * route_gates[step_idx].reshape(-1)[None, :]
        combine_mat = jnp.sum(gate_map.reshape(slot_count, local_req, TOPK), -1)
        mixed_part = jnp.dot(combine_mat.T, expert_flat, precision=HIGHEST)
        hidden_part = lax.dynamic_slice_in_dim(hidden, expert_pos * part_width, part_width, 1)
        outputs.append((hidden_part + mixed_part).astype(jnp.bfloat16))
        if step_idx == 0:
            guest_out = shifted(picked, "dp", data_count // 2)
    return (jnp.stack(outputs), guest_out)


def solution(mesh):
    in_specs = (
        P(None, "dp", None),
        P(None, "dp", None),
        P("dp", None, "expert", None),
        P("dp"),
        P("dp", None),
        P(None, "dp", None),
        P("expert", None),
        P(),
        P(None, "dp", None),
        P(None, "dp", None),
        P("dp", None, "expert"),
        P("dp", None, "expert"),
        P("dp", "expert", None),
    )
    out_specs = (P(None, "dp", "expert"), P("dp", "expert", None))
    return jax.shard_map(shards, mesh=mesh, in_specs=in_specs, out_specs=out_specs, check_vma=False)
```

profile of v0, /device:TPU:2, one launch (start us, length us, event | category | flops | bytes accessed | tf_op | source)
XLA Modules:
  0.0 1028.6 jit_solution(13754432659454517317)
XLA Ops:
  7.2 1.0 slice_bitcast_fusion.10
  8.4 4.0 reshape.328
  12.4 2.7 fusion.135
  16.2 0.5 fusion.138
  17.2 46.2 %all_gather.29 = bf16[8,4,32,128]{3,2,1,0:T(8,128)(2,1)S(1)} all-gather(bf16[1,4,32,128]{3,2,1,0:T(8,128)(2,1)S(1)} %bitcast.265), channel_id=1, replica_groups=mesh['dp'=32,'expert'=8] {'expert'}, dimensions={0}, use_global_device_ids=true | all-gather | bytes 294912 | tf_op jit(solution)/shard_map/all_gather | solution.py:22
  63.5 31.0 %all_gather.28 = bf16[8,4,32]{2,1,0:T(4,128)(2,1)S(1)} all-gather(bf16[1,4,32]{2,1,0:T(4,128)(2,1)S(1)} %convert_element_type.326), channel_id=1, replica_groups=mesh['dp'=32,'expert'=8] {'expert'}, dimensions={0}, use_global_device_ids=true | all-gather | bytes 2304 | tf_op jit(solution)/shard_map/all_gather | solution.py:22
  94.5 22.9 %all_gather.27 = bf16[8,4,32]{2,1,0:T(4,128)(2,1)S(1)} all-gather(bf16[1,4,32]{2,1,0:T(4,128)(2,1)S(1)} %convert_element_type.322), channel_id=1, replica_groups=mesh['dp'=32,'expert'=8] {'expert'}, dimensions={0}, use_global_device_ids=true | all-gather | bytes 2304 | tf_op jit(solution)/shard_map/all_gather | solution.py:22
  117.5 1.1 while.39
  119.6 44.7 %all_gather.26 = bf16[8,4,32,128]{3,2,1,0:T(8,128)(2,1)S(1)} all-gather(bf16[1,4,32,128]{3,2,1,0:T(8,128)(2,1)S(1)} %bitcast.264), channel_id=1, replica_groups=mesh['dp'=32,'expert'=8] {'expert'}, dimensions={0}, use_global_device_ids=true | all-gather | bytes 294912 | tf_op jit(solution)/shard_map/all_gather | solution.py:22
  164.4 28.6 %all_gather.25 = bf16[8,4,32]{2,1,0:T(4,128)(2,1)S(1)} all-gather(bf16[1,4,32]{2,1,0:T(4,128)(2,1)S(1)} %convert_element_type.300), channel_id=1, replica_groups=mesh['dp'=32,'expert'=8] {'expert'}, dimensions={0}, use_global_device_ids=true | all-gather | bytes 2304 | tf_op jit(solution)/shard_map/all_gather | solution.py:22
  193.1 23.1 %all_gather.24 = bf16[8,4,32]{2,1,0:T(4,128)(2,1)S(1)} all-gather(bf16[1,4,32]{2,1,0:T(4,128)(2,1)S(1)} %convert_element_type.296), channel_id=1, replica_groups=mesh['dp'=32,'expert'=8] {'expert'}, dimensions={0}, use_global_device_ids=true | all-gather | bytes 2304 | tf_op jit(solution)/shard_map/all_gather | solution.py:22
  216.2 1.1 while.38
  217.8 3.6 convolution_convert_fusion.4
  221.6 1.3 convolution_convert_fusion.5
  223.2 104.5 %all-reduce.3.cloned.1.call-done = (bf16[4,4096]{1,0:T(4,128)(2,1)}, bf16[4,4096]{1,0:T(4,128)(2,1)}) async-done(((bf16[4,4096]{1,0:T(4,128)(2,1)}, bf16[4,4096]{1,0:T(4,128)(2,1)}), (bf16[4,4096]{1,0:T(4,128)(2,1)}, bf16[4,4096]{1,0:T(4,128)(2,1)})) %all-reduce.3.cloned.1.call-update) | async-done | bytes 65552 | tf_op jit(solution)/shard_map/psum | solution.py:143
  327.7 1.0 multiply_reduce_fusion.1
  328.7 0.9 multiply_convert_fusion.1
  330.0 1.5 reshape.334
  331.5 5.2 all-to-all-start
  337.0 1.4 convolution_convert_fusion.1
  338.4 2.5 reshape.339
  341.0 21.2 %all-to-all-done = bf16[32,2,2,4096]{3,2,1,0:T(2,128)(2,1)S(1)} async-done(((bf16[32,2,2,4096]{3,2,1,0:T(2,128)(2,1)}), bf16[32,2,2,4096]{3,2,1,0:T(2,128)(2,1)S(1)}, u32[]{:S(2)}, u32[]{:S(2)}) %all-to-all-start) | async-done | bytes 1048608 | tf_op jit(solution)/shard_map/all_to_all | solution.py:166
  362.2 1.0 copy-done.2
  363.2 6.4 all-to-all-start.2
  369.6 2.8 fusion.20
  372.4 4.1 fusion.6
  376.5 3.3 copy.51
  379.9 15.2 %all-to-all-done.2 = bf16[32,2,2,4096]{3,2,1,0:T(2,128)(2,1)S(1)} async-done(((bf16[32,2,2,4096]{3,2,1,0:T(2,128)(2,1)}), bf16[32,2,2,4096]{3,2,1,0:T(2,128)(2,1)S(1)}, u32[]{:S(2)}, u32[]{:S(2)}) %all-to-all-start.2) | async-done | bytes 1048608 | tf_op jit(solution)/shard_map/all_to_all | solution.py:166
  395.0 7.1 all-to-all-start.1
  402.4 2.5 fusion.23
  404.9 22.8 %all-to-all-done.1 = bf16[32,2,2,4096]{3,2,1,0:T(2,128)(2,1)} async-done(((bf16[32,2,2,4096]{3,2,1,0:T(2,128)(2,1)}), bf16[32,2,2,4096]{3,2,1,0:T(2,128)(2,1)}, u32[]{:S(2)}, u32[]{:S(2)}) %all-to-all-start.1) | async-done | bytes 1048608 | tf_op jit(solution)/shard_map/all_to_all | solution.py:175
  427.6 125.4 %copy.70 = bf16[32,2,2,4096]{2,1,0,3:T(2,128)(2,1)} copy(bf16[32,2,2,4096]{3,2,1,0:T(2,128)(2,1)} %all-to-all-done.1) | data formatting | bytes 2097152
  553.1 96.7 %reshape.375 = bf16[4096,128]{1,0:T(8,128)(2,1)} reshape(bf16[4096,32,2,2]{3,2,1,0:T(2,128)(2,1)} %bitcast.58) | data formatting | bytes 2097152
  649.8 3.8 fusion.7
  653.6 2.3 copy.54
  655.9 38.1 %all_to_all.20 = bf16[32,2,2,4096]{3,2,1,0:T(2,128)(2,1)S(1)} all-to-all(bf16[32,2,2,4096]{3,2,1,0:T(2,128)(2,1)S(1)} %copy.54), channel_id=1, replica_groups=mesh['dp'=32,'expert'=8] {'dp'}, dimensions={0} | all-to-all | bytes 2097152 | tf_op jit(solution)/shard_map/all_to_all | solution.py:175
  694.0 110.7 %copy.72 = bf16[32,2,2,4096]{2,1,0,3:T(2,128)(2,1)} copy(bf16[32,2,2,4096]{3,2,1,0:T(2,128)(2,1)S(1)} %all_to_all.20) | data formatting | bytes 2097152
  804.7 96.7 %reshape.377 = bf16[4096,128]{1,0:T(8,128)(2,1)} reshape(bf16[4096,32,2,2]{3,2,1,0:T(2,128)(2,1)} %bitcast.60) | data formatting | bytes 2097152
  901.5 2.2 gather_fusion
  903.6 2.6 collective-permute-start
  906.5 4.9 collective-permute-done
  911.4 19.8 %reshape.376 = bf16[512,32,2,2]{3,2,1,0:T(2,128)(2,1)} reshape(bf16[512,128]{1,0:T(8,128)(2,1)} %reduce-scatter.7.cloned.1.call-done) | data formatting | bytes 262144
  931.2 13.1 %reshape.379 = bf16[128,512]{0,1:T(8,128)(2,1)S(1)} reshape(bf16[32,2,2,512]{2,1,0,3:T(2,128)(2,1)} %bitcast.262) | data formatting | bytes 262144 | tf_op jit(solution)/shard_map/reshape | solution.py:181
  944.2 43.4 %reduce-scatter.9.cloned.1.call-done = bf16[512,128]{1,0:T(8,128)(2,1)} async-done(((bf16[4096,128]{1,0:T(8,128)(2,1)}), bf16[512,128]{1,0:T(8,128)(2,1)}) %reduce-scatter.9.cloned.1.call-update) | async-done | bytes 131088
  987.6 19.8 %reshape.378 = bf16[512,32,2,2]{3,2,1,0:T(2,128)(2,1)} reshape(bf16[512,128]{1,0:T(8,128)(2,1)} %reduce-scatter.9.cloned.1.call-done) | data formatting | bytes 262144
  1007.4 13.0 %reshape.380 = bf16[128,512]{0,1:T(8,128)(2,1)S(1)} reshape(bf16[32,2,2,512]{2,1,0,3:T(2,128)(2,1)} %bitcast.263) | data formatting | bytes 262144 | tf_op jit(solution)/shard_map/reshape | solution.py:181
  1020.8 0.6 pad_maximum_fusion
  1021.5 0.7 copy.147
  (114 shorter events, 7.7 us)
Async XLA Ops:
  7.2 365.2 %copy-start = (bf16[2,128,4096]{2,1,0:T(8,128)(2,1)S(1)}, bf16[2,128,4096]{2,1,0:T(8,128)(2,1)}, u32[]{:S(2)}) copy-start(bf16[2,128,4096]{2,1,0:T(8,128)(2,1)} %param.29) | copy-start | bytes 6291460
  7.2 320.5 %all-reduce.3.cloned.1.call-start = ((), (), s32[]{:S(2)}) async-start(), calls=%async_computation.8 | async-start | bytes 131072 | tf_op jit(solution)/shard_map/psum | solution.py:143
  12.4 2.7 copy-start.8
  16.2 102.5 %copy-start.6 = (bf16[2,4,512]{2,1,0:T(4,128)(2,1)S(1)}, bf16[2,4,512]{2,1,0:T(4,128)(2,1)}, u32[]{:S(2)}) copy-start(bf16[2,4,512]{2,1,0:T(4,128)(2,1)} %param.18) | copy-start | bytes 24580
  217.8 3.8 copy-start.1
  221.6 1.3 copy-start.4
  221.6 106.1 %copy-start.3 = (bf16[2,4,4096]{2,1,0:T(4,128)(2,1)S(1)}, bf16[2,4,4096]{2,1,0:T(4,128)(2,1)}, u32[]{:S(2)}) copy-start(bf16[2,4,4096]{2,1,0:T(4,128)(2,1)} %param.22) | copy-start | bytes 196612
  221.6 107.1 %copy-start.5 = (f32[4096]{0:T(1024)S(1)}, f32[4096]{0:T(1024)}, u32[]{:S(2)}) copy-start(f32[4096]{0:T(1024)} %param.24) | copy-start | bytes 49156
  331.5 30.7 %all-to-all-start = ((bf16[32,2,2,4096]{3,2,1,0:T(2,128)(2,1)}), bf16[32,2,2,4096]{3,2,1,0:T(2,128)(2,1)S(1)}, u32[]{:S(2)}, u32[]{:S(2)}) async-start(bf16[32,2,2,4096]{3,2,1,0:T(2,128)(2,1)} %reshape.334), calls=%async_computation | async-start | bytes 2097152 | tf_op jit(solution)/shard_map/all_to_all | solution.py:166
  362.2 1.0 copy-start.2
  363.2 31.8 %all-to-all-start.2 = ((bf16[32,2,2,4096]{3,2,1,0:T(2,128)(2,1)}), bf16[32,2,2,4096]{3,2,1,0:T(2,128)(2,1)S(1)}, u32[]{:S(2)}, u32[]{:S(2)}) async-start(bf16[32,2,2,4096]{3,2,1,0:T(2,128)(2,1)} %reshape.339), calls=%async_computation.2 | async-start | bytes 2097152 | tf_op jit(solution)/shard_map/all_to_all | solution.py:166
  395.0 32.6 %all-to-all-start.1 = ((bf16[32,2,2,4096]{3,2,1,0:T(2,128)(2,1)}), bf16[32,2,2,4096]{3,2,1,0:T(2,128)(2,1)}, u32[]{:S(2)}, u32[]{:S(2)}) async-start(bf16[32,2,2,4096]{3,2,1,0:T(2,128)(2,1)} %copy.51), calls=%async_computation.1 | async-start | bytes 2097152 | tf_op jit(solution)/shard_map/all_to_all | solution.py:175
  402.2 509.2 %reduce-scatter.7.cloned.1.call-start = ((), (), s32[]{:S(2)}) async-start(), calls=%async_computation.6 | async-start | bytes 1179648
  649.8 337.8 %reduce-scatter.9.cloned.1.call-start = ((), (), s32[]{:S(2)}) async-start(), calls=%async_computation.7 | async-start | bytes 1179648
  804.7 96.8 %copy-start.9 = (s32[8,2]{0,1:T(2,128)S(1)}, s32[8,2]{0,1:T(2,128)}, u32[]{:S(2)}) copy-start(s32[8,2]{0,1:T(2,128)} %param.21) | copy-start | bytes 196
  804.7 101.7 %copy-start.7 = (f32[2,4,8]{2,1,0:T(4,128)S(1)}, f32[2,4,8]{2,1,0:T(4,128)}, u32[]{:S(2)}) copy-start(f32[2,4,8]{2,1,0:T(4,128)} %param.26) | copy-start | bytes 772
  903.6 7.7 collective-permute-start
Sparse Core Ops, SparseCore 0:
  223.0 104.6 all-reduce.2
  649.9 85.9 reduce-scatter.6
  901.6 85.9 reduce-scatter.8
where the time goes:
time: 1040 us; the launch traced here: 1030 us
  local copies, waits for them, and re-layouts  517 us (50%)
  blocking collectives  235 us (23%)
  waiting for transfers between devices  212 us (20%)
  matrix products  22.5 us (2%)
  starting transfers between devices  21.6 us (2%)
  between operations  14.1 us (1%)
    unnamed x30, local copies, waits for them, and re-layouts  472 us
    all_gather x6, blocking collectives, combined_all(): lax.all_gather(part.astype(kind), axis)  197 us
    psum x1, waiting for transfers between devices, shards(): lax.psum(jnp.dot(attention, out_weight, preferred_element_type=jnp.float3...  104 us
    unnamed x5, waiting for transfers between devices  43.4 us
    all_to_all x1, blocking collectives, shards(): lax.all_to_all(produced.astype(jnp.bfloat16), 'dp', split_axis=0, concat_...  38.1 us
    all_to_all x2, waiting for transfers between devices, shards(): lax.all_to_all(outgoing, 'dp', split_axis=0, concat_axis=0, tiled=True)  36.4 us
    reshape x2, local copies, waits for them, and re-layouts, shards(): expert_flat = expert_out.reshape(slot_count, part_width).astype(jnp.float32)  26.1 us
    all_to_all x1, waiting for transfers between devices, shards(): lax.all_to_all(produced.astype(jnp.bfloat16), 'dp', split_axis=0, concat_...  22.8 us
  transfers between devices with their start and end apart: 7, of which 6 were waited for; matrix products, arithmetic and copies ran while one was open for 26% of the time, Pallas kernels for 0%

commit v1 on v0

v1 whole, which is shorter than its diff:
```python
import math

import jax
import jax.numpy as jnp
from jax import lax
from jax.sharding import PartitionSpec as P

HD = 128
QH = 32
KVH = 2
TOPK = 8
BLOCKS = 32
EXPERTS = 64


def shards(
    queries,
    fresh_entries,
    cache_blocks,
    lengths,
    migration,
    residual,
    out_weight,
    norm_gain,
    routes,
    route_gates,
    w_gate,
    w_up,
    w_down,
):
    n_p = lax.axis_size("expert")
    n_dp = lax.axis_size("dp")
    pos = lax.axis_index("expert")
    me = lax.axis_index("dp")
    reqs = cache_blocks.shape[0]
    rows = cache_blocks.shape[2]
    groups = QH // KVH
    own = QH // n_p
    width = out_weight.shape[1]
    part = width // n_p
    tokens = 2 * reqs
    scale = 1.0 / math.sqrt(HD)

    picked = cache_blocks[migration[:, 0], migration[:, 1]]
    half = n_dp // 2
    guest = lax.ppermute(picked, "dp", [(s, (s + half) % n_dp) for s in range(n_dp)])

    expert_ids = jnp.arange(EXPERTS, dtype=jnp.int32)
    coef = jnp.sum(
        jnp.where(routes[..., None] == expert_ids, route_gates[..., None], 0.0), 2
    ).reshape(tokens, EXPERTS)
    coef_all = lax.all_gather(coef, "dp").reshape(n_dp * tokens, EXPERTS)

    positions = (
        jnp.arange(BLOCKS, dtype=jnp.int32)[:, None] * (rows * n_p)
        + pos * rows
        + jnp.arange(rows, dtype=jnp.int32)[None, :]
    ).reshape(-1)
    valid = positions[None, :] < lengths[:, None]
    stored = cache_blocks.reshape(reqs, BLOCKS * rows, 2, KVH, HD)
    q = queries.reshape(2, reqs, KVH, groups, HD)
    scores = (
        jnp.einsum("srkgd,rpkd->rksgp", q, stored[:, :, 0], preferred_element_type=jnp.float32)
        * scale
    )
    scores = jnp.where(valid[:, None, None, None, :], scores, -jnp.inf)
    peak = jnp.max(scores, -1)
    weights = jnp.exp(scores - peak[..., None])
    total = jnp.sum(weights, -1)
    weighted = jnp.einsum(
        "rksgp,rpkd->rksgd",
        weights.astype(jnp.bfloat16),
        stored[:, :, 1],
        preferred_element_type=jnp.float32,
    )

    def to_owner(v):
        v = jnp.moveaxis(v, 2, 0).reshape((2, reqs, n_p, own) + v.shape[4:])
        return jnp.moveaxis(v, 2, 0)

    state = to_owner(weighted).astype(jnp.bfloat16)
    stats = jnp.stack([to_owner(peak), to_owner(total)], -1)
    state = lax.all_to_all(state, "expert", 0, 0, tiled=True).astype(jnp.float32)
    stats = lax.all_to_all(stats, "expert", 0, 0, tiled=True)
    peaks, totals = stats[..., 0], stats[..., 1]

    kv = pos * own // groups
    fresh = fresh_entries.reshape(2, reqs, 2, KVH, HD).astype(jnp.float32)
    fresh = lax.dynamic_index_in_dim(fresh, kv, 3, keepdims=False)
    q_own = lax.dynamic_slice_in_dim(
        queries.reshape(2, reqs, QH, HD), pos * own, own, 2
    ).astype(jnp.float32)
    f_scores = jnp.sum(q_own[:, None] * fresh[None, :, :, 0][:, :, :, None], -1) * scale
    seen = jnp.arange(2)[None, :] <= jnp.arange(2)[:, None]
    f_scores = jnp.where(seen[:, :, None, None], f_scores, -jnp.inf)
    top = jnp.maximum(jnp.max(peaks, 0), jnp.max(f_scores, 1))
    w_dev = jnp.exp(peaks - top)
    f_w = jnp.exp(f_scores - top[:, None])
    denom = jnp.sum(w_dev * totals, 0) + jnp.sum(f_w, 1)
    numer = jnp.sum(w_dev[..., None] * state, 0) + jnp.sum(
        f_w[..., None] * fresh[None, :, :, 1][:, :, :, None], 1
    )
    attention = (numer / denom[..., None]).astype(jnp.bfloat16).reshape(tokens, own * HD)
    projected = jnp.dot(attention, out_weight, preferred_element_type=jnp.float32)
    projected = lax.psum_scatter(
        projected.astype(jnp.bfloat16), "expert", scatter_dimension=1, tiled=True
    ).astype(jnp.float32)
    res = lax.dynamic_slice_in_dim(residual.reshape(tokens, width), pos * part, part, 1)
    hidden = res.astype(jnp.float32) + projected

    gathered = lax.all_gather(hidden.astype(jnp.bfloat16), ("dp", "expert"))
    gathered = jnp.moveaxis(gathered.reshape(n_dp, n_p, tokens, part), 1, 2)
    gathered = gathered.reshape(n_dp * tokens, width).astype(jnp.float32)
    spread = jnp.mean(gathered * gathered, -1, keepdims=True)
    normed = (gathered * lax.rsqrt(spread + 1e-06) * norm_gain).astype(jnp.bfloat16)
    gate = jnp.einsum("td,jdf->tjf", normed, w_gate, preferred_element_type=jnp.float32)
    up = jnp.einsum("td,jdf->tjf", normed, w_up, preferred_element_type=jnp.float32)
    n_e = w_gate.shape[0]
    coef_own = lax.dynamic_slice_in_dim(coef_all, me * n_e, n_e, 1)
    act = (jax.nn.silu(gate) * up * coef_own[..., None]).astype(jnp.bfloat16)
    mixed = jnp.dot(
        act.reshape(n_dp * tokens, -1),
        w_down.reshape(-1, width),
        preferred_element_type=jnp.float32,
    ).astype(jnp.bfloat16)
    mixed = jnp.moveaxis(mixed.reshape(n_dp, tokens, n_p, part), 2, 1)
    mixed = mixed.reshape(n_dp * n_p, tokens, part)
    mixed = lax.psum_scatter(mixed, ("dp", "expert"), scatter_dimension=0)
    out = (hidden + mixed.astype(jnp.float32)).astype(jnp.bfloat16)
    return (out.reshape(2, reqs, part), guest)


def solution(mesh):
    in_specs = (
        P(None, "dp", None),
        P(None, "dp", None),
        P("dp", None, "expert", None),
        P("dp"),
        P("dp", None),
        P(None, "dp", None),
        P("expert", None),
        P(),
        P(None, "dp", None),
        P(None, "dp", None),
        P("dp", None, "expert"),
        P("dp", None, "expert"),
        P("dp", "expert", None),
    )
    out_specs = (P(None, "dp", "expert"), P("dp", "expert", None))
    return jax.shard_map(shards, mesh=mesh, in_specs=in_specs, out_specs=out_specs, check_vma=False)
```

time: 1040 us -> 2200 us (2.12)
  waiting for transfers between devices: 212 us -> 2100 us
  local copies, waits for them, and re-layouts: 517 us -> 15.9 us
  blocking collectives: 235 us -> 34.1 us
    reduce_scatter x0 -> x2, waiting for transfers between devices: none -> 1420 us  [the longest x1 1340 us: shards(): mixed = lax.psum_scatter(mixed, ('dp', 'expert'), scatter_dimension=0)]
    all_gather x0 -> x1, waiting for transfers between devices: none -> 656 us  [shards(): gathered = lax.all_gather(hidden.astype(jnp.bfloat16), ('dp', 'expert'))]
    unnamed x30 -> x25, local copies, waits for them, and re-layouts: 472 us -> 3.29 us
    all_gather x6 -> x1, blocking collectives: 197 us -> 34.1 us  [shards(): coef_all = lax.all_gather(coef, 'dp').reshape(n_dp * tokens, EXPERTS)]
    psum x1 -> x0, waiting for transfers between devices: 104 us -> none  [shards(): lax.psum(jnp.dot(attention, out_weight, preferred_element_type=jnp.float3...]
    unnamed x5 -> x3, waiting for transfers between devices: 43.4 us -> 0.05 us
    all_to_all x3 -> x2, waiting for transfers between devices: 59.2 us -> 17.5 us  [the longest x1 9.84 us: shards(): lax.all_to_all(state, 'expert', 0, 0, tiled=True).astype(jnp.float32)]
    all_to_all x1 -> x0, blocking collectives: 38.1 us -> none  [shards(): lax.all_to_all(produced.astype(jnp.bfloat16), 'dp', split_axis=0, concat_...]
  transfers between devices with their start and end apart: 7 -> 6, of which waited for: 6 -> 6; matrix products, arithmetic and copies ran while one was open for 26% -> 0% of each run, Pallas kernels for 0% -> 0%
where the time goes in v1:
time: 2200 us
  waiting for transfers between devices  2100 us (95%)
  blocking collectives  34.1 us (2%)
    reduce_scatter x1, waiting for transfers between devices, shards(): mixed = lax.psum_scatter(mixed, ('dp', 'expert'), scatter_dimension=0)  1340 us
    all_gather x1, waiting for transfers between devices, shards(): gathered = lax.all_gather(hidden.astype(jnp.bfloat16), ('dp', 'expert'))  656 us
    reduce_scatter x1, waiting for transfers between devices, shards(): lax.psum_scatter(projected.astype(jnp.bfloat16), 'expert', scatter_dimens...  78.2 us
  transfers between devices with their start and end apart: 6, of which 6 were waited for; matrix products, arithmetic and copies ran while one was open for 0% of the time, Pallas kernels for 0%

profile of v1, /device:TPU:2, one launch (start us, length us, event | category | flops | bytes accessed | tf_op | source)
XLA Modules:
  0.0 2196.2 jit_solution(6509600560720681328)
XLA Ops:
  7.2 0.1 iota_add_fusion
  7.3 0.1 add.97
  7.3 4.1 reshape.163
  11.4 3.7 fusion.41
  15.1 0.1 reshape.162
  15.2 0.1 broadcast_compare_fusion
  15.3 1.8 fusion.43
  17.1 0.3 fusion.7
  17.3 0.1 reshape.165
  17.4 0.1 reshape.164
  17.5 0.6 copy.47
  18.2 11.1 all-to-all-start
  29.3 0.1 reshape.166
  29.5 1.6 fusion.5
  31.0 0.1 multiply_reduce_fusion.3
  31.1 0.1 fusion.32
  31.2 0.7 copy.52
  31.9 7.6 all-to-all-done
  39.5 3.4 all-to-all-start.1
  43.0 0.1 fusion.40
  43.1 0.1 multiply_reduce_fusion.2
  43.2 9.8 all-to-all-done.1
  53.1 0.1 multiply_reduce_fusion.1
  53.2 0.1 fusion.28
  53.3 3.5 convolution_convert_fusion
  56.9 78.2 %reduce-scatter.3.cloned.1.call-done = bf16[8,512]{1,0:T(8,128)(2,1)} async-done(((bf16[8,4096]{1,0:T(8,128)(2,1)}), bf16[8,512]{1,0:T(8,128)(2,1)}) %reduce-scatter.3.cloned.1.call-update) | async-done | bytes 8208 | tf_op jit(solution)/shard_map/reduce_scatter | solution.py:105
  135.1 1.3 fusion.29
  136.4 0.0 reduce-scatter.5.cloned.1.call-start
  136.5 0.1 select_reduce_fusion
  136.6 34.1 %all_gather.11 = f32[32,8,64]{2,1,0:T(8,128)S(1)} all-gather(f32[1,8,64]{2,1,0:T(8,128)S(1)} %bitcast.102), channel_id=1, replica_groups=mesh['dp'=32,'expert'=8] {'dp'}, dimensions={0}, use_global_device_ids=true | all-gather | bytes 67584 | tf_op jit(solution)/shard_map/all_gather | solution.py:52
  170.7 0.1 constant_dynamic-slice_fusion
  170.8 0.1 copy.53
  170.8 655.6 %all-gather.3.cloned.1.call-done = bf16[2048,512]{1,0:T(8,128)(2,1)} async-done(((bf16[8,512]{1,0:T(8,128)(2,1)}), bf16[2048,512]{1,0:T(8,128)(2,1)}) %all-gather.3.cloned.1.call-update) | async-done | bytes 2097168 | tf_op jit(solution)/shard_map/all_gather | solution.py:111
  826.4 2.1 multiply_reduce_fusion
  828.5 0.1 reduce_sum.86
  828.7 0.1 rsqrt.12
  828.8 2.3 convert_element_type.113
  831.1 1.9 copy-done.1
  833.0 0.8 fusion.20
  833.8 6.6 fusion
  840.5 0.7 copy-done.11
  841.2 2.2 gather_fusion
  843.3 0.1 collective-permute-start
  843.4 6.5 collective-permute-done
  849.9 1337.8 %reduce-scatter.5.cloned.1.call-done = bf16[1,8,512]{2,1,0:T(8,128)(2,1)} async-done(((bf16[256,8,512]{2,1,0:T(8,128)(2,1)}), bf16[1,8,512]{2,1,0:T(8,128)(2,1)}) %reduce-scatter.5.cloned.1.call-update) | async-done | bytes 8208 | tf_op jit(solution)/shard_map/reduce_scatter | solution.py:128
  2187.7 0.7 fusion.27
  2188.4 0.6 reshape.170
  2189.0 0.7 copy.76
  (46 shorter events, 0.4 us)
Async XLA Ops:
  7.2 826.7 %copy-start = (bf16[2,128,4096]{2,1,0:T(8,128)(2,1)S(1)}, bf16[2,128,4096]{2,1,0:T(8,128)(2,1)}, u32[]{:S(2)}) copy-start(bf16[2,128,4096]{2,1,0:T(8,128)(2,1)} %param.25) | copy-start | bytes 6291460
  11.4 3.7 copy-start.3
  11.4 3.8 copy-start.10
  15.1 14.3 copy-start.7
  18.2 21.4 all-to-all-start
  39.5 13.5 all-to-all-start.1
  42.9 92.2 %reduce-scatter.3.cloned.1.call-start = ((), (), s32[]{:S(2)}) async-start(), calls=%async_computation.4 | async-start | bytes 73728 | tf_op jit(solution)/shard_map/reduce_scatter | solution.py:105
  53.3 3.6 copy-start.5
  53.3 83.2 %copy-start.8 = (f32[2,4,8]{2,1,0:T(4,128)S(1)}, f32[2,4,8]{2,1,0:T(4,128)}, u32[]{:S(2)}) copy-start(f32[2,4,8]{2,1,0:T(4,128)} %param.22) | copy-start | bytes 772
  53.3 83.2 %copy-start.9 = (s32[2,4,8]{2,1,0:T(4,128)S(1)}, s32[2,4,8]{2,1,0:T(4,128)}, u32[]{:S(2)}) copy-start(s32[2,4,8]{2,1,0:T(4,128)} %param.21) | copy-start | bytes 772
  56.9 769.6 %all-gather.3.cloned.1.call-start = ((), (), s32[]{:S(2)}) async-start(), calls=%async_computation.6 | async-start | bytes 2105344 | tf_op jit(solution)/shard_map/all_gather | solution.py:111
  136.4 2051.3 %reduce-scatter.5.cloned.1.call-start = ((), (), s32[]{:S(2)}) async-start(), calls=%async_computation.5 | async-start | bytes 2105344 | tf_op jit(solution)/shard_map/reduce_scatter | solution.py:128
  828.7 4.3 copy-start.2
  828.8 4.3 copy-start.4
  831.1 1.9 copy-start.1
  840.5 0.7 copy-start.11
  840.5 1347.2 %copy-start.6 = (bf16[8,512]{1,0:T(8,128)(2,1)S(1)}, bf16[8,512]{1,0:T(8,128)(2,1)}, u32[]{:S(2)}) copy-start(bf16[8,512]{1,0:T(8,128)(2,1)} %reduce-scatter.3.cloned.1.call-done) | copy-start | bytes 24580
  843.3 6.6 collective-permute-start
Sparse Core Ops, SparseCore 0:
  57.0 78.0 reduce-scatter.2
  137.5 688.8 all-gather.2
  840.6 1347.0 reduce-scatter.4

commit v2 on v1

v2 whole, which is shorter than its diff:
```python
import functools
import math

import jax
import jax.numpy as jnp
from jax import lax
from jax.experimental import pallas as pl
from jax.experimental.pallas import tpu as pltpu
from jax.sharding import PartitionSpec as P

MESH = pl.DeviceIdType.MESH
HD = 128
QH = 32
KVH = 2
TOPK = 8
BLOCKS = 32
NX, NZL, NY, NZH = 4, 4, 4, 2
N_P = NY * NZH
N_Z = NZH * NZL
N_DP = NX * NZL * 2
REQS = 4
TOK = 2 * REQS
D = 4096
PART = D // N_P
HALF = PART // 2
ROWS = 16
POSN = BLOCKS * ROWS
OWN = QH // N_P
ALL = N_DP * TOK
F32 = jnp.float32
BF16 = jnp.bfloat16
NEG = -1e30
N_SEMS = 72
MIB = 1024 * 1024


def kernel(
    q_ref,
    fresh_ref,
    cache_ref,
    len_ref,
    mig_ref,
    res_ref,
    ow_ref,
    gain_ref,
    routes_ref,
    gates_ref,
    wg_ref,
    wu_ref,
    wd_ref,
    out_ref,
    guest_ref,
    cache_v,
    ow_v,
    wgu_v,
    wd_v,
    picked_v,
    q_s,
    q_b,
    f_s,
    r_s,
    a_send,
    a_recv,
    b_send,
    b_recv,
    hid,
    rt,
    g_buf,
    acc,
    ssq,
    act,
    p_buf,
    s_buf,
    m_buf,
    a_in,
    a_mid,
    n_buf,
    b_in,
    b_mid,
    n2_buf,
    z_send,
    z_recv,
    o_s,
    load_sem,
    send_sem,
    recv_sem,
):
    me = lax.axis_index("dp")
    p = lax.axis_index("expert")
    core = lax.rem(me, 2)
    zlo = lax.rem(lax.div(me, 2), NZL)
    x = lax.div(me, 2 * NZL)
    y = lax.div(p, NZH)
    zhi = lax.rem(p, NZH)
    z = zhi * NZL + zlo

    def place(x_, y_, zlo_, zhi_, core_):
        return ((x_ * NZL + zlo_) * 2 + core_, y_ * NZH + zhi_)

    def at_p(k):
        return (me, lax.rem(p + k, N_P))

    def at_z(k):
        t = lax.rem(z + k, N_Z)
        return place(x, y, lax.rem(t, NZL), lax.div(t, NZL), core)

    def at_x(k):
        return place(lax.rem(x + k, NX), y, zlo, zhi, core)

    def at_zlo(k):
        return place(x, y, lax.rem(zlo + k, NZL), zhi, core)

    def at_a(k):
        return place(lax.rem(x + (1 - core) * k, NX), lax.rem(y + core * k, NY), zlo, zhi, core)

    def at_b(k):
        return place(lax.rem(x + core * k, NX), lax.rem(y + (1 - core) * k, NY), zlo, zhi, core)

    sibling = place(x, y, zlo, zhi, 1 - core)
    ia = (1 - core) * x + core * y
    ib = core * x + (1 - core) * y
    sib_ia = core * x + (1 - core) * y

    loads = []

    def load(src, dst):
        cp = pltpu.make_async_copy(src, dst, load_sem.at[len(loads)])
        cp.start()
        loads.append(cp)
        return cp

    cache_cp = [load(cache_ref.at[r], cache_v.at[r]) for r in range(REQS)]
    ow_cp = load(ow_ref, ow_v)
    w_cp = []
    for j in range(2):
        w_cp.append(load(wg_ref.at[j], wgu_v.at[:, pl.ds(256 * j, 128)]))
        w_cp.append(load(wu_ref.at[j], wgu_v.at[:, pl.ds(256 * j + 128, 128)]))
    wd_cp = [load(wd_ref.at[j], wd_v.at[pl.ds(128 * j, 128)]) for j in range(2)]

    barrier = pltpu.get_barrier_semaphore()
    peers = [at_p(k) for k in range(1, N_P)]
    peers += [at_z(k) for k in range(1, N_Z) if k != NZL]
    peers += [at_x(k) for k in range(1, NX)]
    peers += [sibling]
    for peer in peers:
        pl.semaphore_signal(barrier, inc=1, device_id=peer, device_id_type=MESH)

    sent = []

    def send(src, dst, peer):
        k = len(sent)
        cp = pltpu.make_async_remote_copy(
            src_ref=src,
            dst_ref=dst,
            send_sem=send_sem.at[k],
            recv_sem=recv_sem.at[k],
            device_id=peer,
            device_id_type=MESH,
        )
        cp.start()
        sent.append(cp)
        return cp

    lane = lax.broadcasted_iota(jnp.int32, (REQS, 128), 1)
    for s in range(2):
        ids = routes_ref[s]
        vals = gates_ref[s]
        coef = jnp.zeros((REQS, 128), F32)
        for k in range(TOPK):
            coef = coef + jnp.where(lane == ids[:, k : k + 1], vals[:, k : k + 1], 0.0)
        rt[core, x, zlo, pl.ds(REQS * s, REQS), :] = coef

    for s in range(2):
        q_s[pl.ds(REQS * s, REQS), :] = q_ref[s].astype(F32)
        r_s[pl.ds(REQS * s, REQS), :] = res_ref[
            s, :, pl.ds(pl.multiple_of(p * PART, PART), PART)
        ].astype(F32)
    q_b[...] = jnp.concatenate(
        [q_s[:, h * HD : (h + 1) * HD] for h in range(QH)], axis=0
    ).astype(BF16)

    for cp in cache_cp:
        cp.wait()
    for m in range(8):
        picked_v[m] = cache_v[mig_ref[m, 0], mig_ref[m, 1]]

    scale = 1.0 / math.sqrt(HD)
    col = lax.broadcasted_iota(jnp.int32, (TOK, POSN), 1)
    row = lax.rem(lax.broadcasted_iota(jnp.int32, (TOK, POSN), 0), REQS)
    position = lax.div(col, ROWS) * (ROWS * N_P) + p * ROWS + lax.rem(col, ROWS)
    limit = jnp.full((TOK, POSN), 0, jnp.int32)
    for r in range(REQS):
        limit = jnp.where(row == r, len_ref[r], limit)
    valid = position < limit
    hk = QH // KVH * TOK
    rid = lax.rem(lax.broadcasted_iota(jnp.int32, (hk, POSN), 0), REQS)
    rid_o = lax.rem(lax.broadcasted_iota(jnp.int32, (hk, HD), 0), REQS)
    sub = lax.broadcasted_iota(jnp.int32, (OWN * TOK, 128), 0)
    lan = lax.broadcasted_iota(jnp.int32, (OWN * TOK, 128), 1)
    for k in range(KVH):
        qk = q_b[k * hk : (k + 1) * hk]
        scores = None
        for r in range(REQS):
            keys = cache_v[r, :, :, k * HD : (k + 1) * HD].reshape(POSN, HD)
            part = lax.dot_general(
                qk, keys, (((1,), (1,)), ((), ())), preferred_element_type=F32
            )
            scores = part if r == 0 else jnp.where(rid == r, part, scores)
        scores = scores.reshape(hk // TOK, TOK, POSN)
        scores = jnp.where(valid[None], scores * scale, NEG)
        peak = jnp.max(scores, -1, keepdims=True).astype(BF16).astype(F32)
        weights = jnp.exp(scores - peak)
        total = jnp.sum(weights, -1, keepdims=True)
        weights = weights.reshape(hk, POSN).astype(BF16)
        state = None
        for r in range(REQS):
            vals = cache_v[r, :, :, (KVH + k) * HD : (KVH + k + 1) * HD].reshape(POSN, HD)
            part = jnp.dot(weights, vals, preferred_element_type=F32)
            state = part if r == 0 else jnp.where(rid_o == r, part, state)
        peak = peak.reshape(hk, 1)
        total = total.reshape(hk, 1)
        total_hi = total.astype(BF16).astype(F32)
        total_lo = total - total_hi
        n_rows = OWN * TOK
        for i in range(hk // n_rows):
            dest = k * (hk // n_rows) + i
            rows = slice(i * n_rows, (i + 1) * n_rows)
            a_send[dest, 0:n_rows, :] = state[rows].astype(BF16)
            stat = jnp.where(lan == sub, peak[rows], 0.0)
            stat = jnp.where(lan == sub + n_rows, total_hi[rows], stat)
            stat = jnp.where(lan == sub + 2 * n_rows, total_lo[rows], stat)
            stat = jnp.sum(stat, axis=0, keepdims=True)
            a_send[dest, n_rows : n_rows + 16, :] = jnp.broadcast_to(stat, (16, 128)).astype(BF16)

    pl.semaphore_wait(barrier, len(peers))

    a_cp = []
    for k in range(1, N_P):
        a_cp.append(send(a_send.at[lax.rem(p + k, N_P)], a_recv.at[k], at_p(k)))
    rt_cp = [
        send(rt.at[core, x, zlo], rt.at[core, x, zlo], at_zlo(k)) for k in range(1, NZL)
    ]
    guest_cp = send(picked_v, guest_ref, at_x(2))
    a_recv[0] = a_send[p]

    kv = lax.div(p, N_P // KVH)
    for n in range(2):
        for j in range(2):
            new = fresh_ref[
                n, :, pl.ds(pl.multiple_of((j * KVH + kv) * HD, HD), HD)
            ].astype(F32)
            f_s[n, j, 0:REQS, :] = new
            f_s[n, j, REQS:TOK, :] = new
    q_own = q_s[:, pl.ds(pl.multiple_of(p * PART, PART), PART)]
    q_own = jnp.stack([q_own[:, i * HD : (i + 1) * HD] for i in range(OWN)], axis=0)
    f_scores = [
        jnp.sum(q_own * f_s[n, 0][None], -1, keepdims=True) * scale for n in range(2)
    ]
    step_row = lax.broadcasted_iota(jnp.int32, (OWN, TOK, 1), 1)
    f_scores[1] = jnp.where(step_row >= REQS, f_scores[1], NEG)

    for cp in a_cp:
        cp.wait_recv()
    n_rows = OWN * TOK
    peaks, totals = [], []
    for k in range(N_P):
        stat = a_recv[k, n_rows : n_rows + 16, :].astype(F32)[0:1]
        peaks.append(jnp.sum(jnp.where(lan == sub, stat, 0.0), -1, keepdims=True))
        in_total = (lan == sub + n_rows) | (lan == sub + 2 * n_rows)
        totals.append(jnp.sum(jnp.where(in_total, stat, 0.0), -1, keepdims=True))
    f_scores = [f.reshape(n_rows, 1) for f in f_scores]
    top = jnp.maximum(f_scores[0], f_scores[1])
    for k in range(N_P):
        top = jnp.maximum(top, peaks[k])
    denom = jnp.zeros((n_rows, 1), F32)
    numer = jnp.zeros((n_rows, HD), F32)
    for n in range(2):
        w = jnp.exp(f_scores[n] - top)
        denom = denom + w
        vals = jnp.broadcast_to(f_s[n, 1][None], (OWN, TOK, HD)).reshape(n_rows, HD)
        numer = numer + w * vals
    for k in range(N_P):
        w = jnp.exp(peaks[k] - top)
        denom = denom + w * totals[k]
        numer = numer + w * a_recv[k, 0:n_rows, :].astype(F32)
    attention = (numer / denom).reshape(OWN, TOK, HD)
    attention = jnp.concatenate([attention[i] for i in range(OWN)], axis=1).astype(BF16)

    for cp in rt_cp:
        cp.wait_recv()
    rt_cp = [send(rt.at[core, x], rt.at[core, x], at_x(k)) for k in range(1, NX)]

    def packed(v):
        return jnp.concatenate([v[:, 0:HALF], v[:, HALF:PART]], axis=0)

    def unpacked(v):
        return jnp.concatenate([v[0:TOK], v[TOK : 2 * TOK]], axis=1)

    ow_cp.wait()
    b_cp = []
    for k in range(1, N_P + 1):
        pp = lax.rem(p + k, N_P)
        term = jnp.dot(
            attention,
            ow_v[:, pl.ds(pl.multiple_of(pp * PART, PART), PART)],
            preferred_element_type=F32,
        )
        if k < N_P:
            b_send[k] = packed(term).astype(BF16)
            b_cp.append(send(b_send.at[k], b_recv.at[k], at_p(k)))
    for cp in rt_cp:
        cp.wait_recv()
    rt_cp = [send(rt.at[core], rt.at[core], sibling)]
    hidden = packed(r_s[...] + term)
    for k in range(1, N_P):
        b_cp[k - 1].wait_recv()
        hidden = hidden + b_recv[k].astype(F32)
    hid[...] = hidden
    g_buf[core, ia, ib, z] = hidden.astype(BF16)

    mine = g_buf.at[core, ia, ib, z]
    z_cp = [send(mine, mine, at_z(k)) for k in range(1, N_Z)]
    for cp in z_cp:
        cp.wait_recv()

    def ring_gather(ref, i, n, at):
        lo, hi = pl.ds(0, n // 2), pl.ds(n // 2, n // 2)
        left = lax.rem(i + 3, 4)
        right = lax.rem(i + 1, 4)
        r_lo = send(ref.at[i, lo], ref.at[i, lo], at(1))
        l_hi = send(ref.at[i, hi], ref.at[i, hi], at(3))
        r_hi = send(ref.at[i, hi], ref.at[i, hi], at(1))
        l_lo = send(ref.at[i, lo], ref.at[i, lo], at(3))
        r_lo.wait_recv()
        f_lo = send(ref.at[left, lo], ref.at[left, lo], at(1))
        l_hi.wait_recv()
        f_hi = send(ref.at[right, hi], ref.at[right, hi], at(3))
        return (r_hi, l_lo, f_lo, f_hi)

    def ring_wait(cps):
        for cp in cps:
            cp.wait_recv()

    ring_wait(ring_gather(g_buf.at[core, ia], ib, N_Z, at_b))
    plane = g_buf.at[core]
    rest = ring_gather(plane, ia, 4, at_a)

    def across(j):
        return send(plane.at[j], plane.at[j], sibling)

    c_cp = [across(ia)]
    rest[0].wait_recv()
    c_cp.append(across(lax.rem(ia + 3, 4)))
    rest[1].wait_recv()
    c_cp.append(across(lax.rem(ia + 1, 4)))
    ring_wait(rest[2:])
    c_cp.append(across(lax.rem(ia + 2, 4)))
    ring_wait(c_cp)
    ring_wait(rt_cp)

    for cp in w_cp:
        cp.wait()
    acc[...] = jnp.zeros_like(acc)
    ssq[...] = jnp.zeros_like(ssq)

    def up_step(i, _):
        yy, zz = lax.div(i, NZH), lax.rem(i, NZH)
        zs = pl.ds(pl.multiple_of(zz * NZL, NZL), NZL)
        halves = []
        for blocks in (g_buf[0, :, yy, zs], g_buf[1, yy, :, zs]):
            blocks = blocks.astype(F32).reshape(NX * NZL, 2 * TOK, HALF)
            halves.append(
                jnp.concatenate(
                    [
                        blocks[:, 0:TOK].reshape(ALL // 2, HALF),
                        blocks[:, TOK : 2 * TOK].reshape(ALL // 2, HALF),
                    ],
                    axis=1,
                )
            )
        rows = jnp.concatenate(halves, axis=0)
        sq = rows * rows
        ssq[...] += (sq[:, 0:128] + sq[:, 128:256]) + (sq[:, 256:384] + sq[:, 384:512])
        at = pl.ds(pl.multiple_of(i * PART, PART), PART)
        rows = (rows * gain_ref[:, at]).astype(BF16)
        acc[...] += jnp.dot(rows, wgu_v[at, :], preferred_element_type=F32)
        return 0

    lax.fori_loop(0, N_P, up_step, 0)
    spread = jnp.sum(ssq[...], -1, keepdims=True) * (1.0 / D)
    norm = lax.rsqrt(spread + 1e-06)
    coefs = rt[...].reshape(ALL, 128)
    lane = lax.broadcasted_iota(jnp.int32, (ALL, 128), 1)
    for j in range(2):
        coef = jnp.sum(jnp.where(lane == 2 * me + j, coefs, 0.0), -1, keepdims=True)
        gate = acc[:, 256 * j : 256 * j + 128] * norm
        up = acc[:, 256 * j + 128 : 256 * j + 256] * norm
        inner = gate / (1.0 + jnp.exp(-gate)) * up
        act[:, 128 * j : 128 * j + 128] = (inner * coef).astype(BF16)

    for cp in wd_cp:
        cp.wait()

    def down_step(i, _):
        yy, zz = lax.div(i, NZH), lax.rem(i, NZH)
        zs = pl.ds(pl.multiple_of(zz * NZL, NZL), NZL)
        at = pl.ds(pl.multiple_of(i * PART, PART), PART)
        made = jnp.dot(act[...], wd_v[:, at], preferred_element_type=F32)
        made = made.reshape(2, NX * NZL, TOK, PART)
        made = jnp.concatenate([made[..., 0:HALF], made[..., HALF:PART]], axis=2)
        made = made.astype(BF16).reshape(2, NX, NZL, 2 * TOK, HALF)
        p_buf[0, :, yy, zs] = made[0]
        p_buf[1, yy, :, zs] = made[1]
        return 0

    lax.fori_loop(0, N_P, down_step, 0)

    order = (2, 1, 3, 0)
    c_cp = []
    for k in order:
        j = lax.rem(sib_ia + k, 4)
        c_cp.append(send(p_buf.at[1 - core, j], s_buf.at[j], sibling))
    for cp, k in zip(c_cp, order):
        cp.wait_recv()
        j = lax.rem(ia + k, 4)
        m_buf[j] = (p_buf[core, j].astype(F32) + s_buf[j].astype(F32)).astype(BF16)

    def ring_sum(ref, i, n, at, arrive, mid):
        half = n // 2
        lo, hi = pl.ds(0, half), pl.ds(half, half)
        left, right, far = lax.rem(i + 3, 4), lax.rem(i + 1, 4), lax.rem(i + 2, 4)
        c_a = send(ref.at[far, lo], arrive.at[0], at(1))
        c_b = send(ref.at[far, hi], arrive.at[1], at(3))
        c_c = send(ref.at[right, hi], arrive.at[2], at(1))
        c_d = send(ref.at[left, lo], arrive.at[3], at(3))
        c_a.wait_recv()
        mid[0] = (ref[right, lo].astype(F32) + arrive[0].astype(F32)).astype(BF16)
        c_e = send(mid.at[0], arrive.at[4], at(1))
        c_b.wait_recv()
        mid[1] = (ref[left, hi].astype(F32) + arrive[1].astype(F32)).astype(BF16)
        c_f = send(mid.at[1], arrive.at[5], at(3))
        c_d.wait_recv()
        c_e.wait_recv()
        low = ref[i, lo].astype(F32) + arrive[3].astype(F32) + arrive[4].astype(F32)
        c_c.wait_recv()
        c_f.wait_recv()
        high = ref[i, hi].astype(F32) + arrive[2].astype(F32) + arrive[5].astype(F32)
        return low, high

    low, high = ring_sum(m_buf, ia, 4, at_a, a_in, a_mid)
    n_buf[0:2] = low.astype(BF16)
    n_buf[2:4] = high.astype(BF16)
    low, high = ring_sum(n_buf, ib, N_Z, at_b, b_in, b_mid)
    n2_buf[0:4] = low
    n2_buf[4:8] = high
    z_send[...] = n2_buf[...].astype(BF16)
    z_cp = [
        send(z_send.at[lax.rem(z + k, N_Z)], z_recv.at[k], at_z(k)) for k in range(1, N_Z)
    ]
    result = hid[...] + n2_buf[z]
    for k in range(1, N_Z):
        z_cp[k - 1].wait_recv()
        result = result + z_recv[k].astype(F32)
    o_s[...] = unpacked(result)
    for s in range(2):
        out_ref[s] = o_s[REQS * s : REQS * (s + 1), :].astype(BF16)
    guest_cp.wait_recv()
    for cp in sent:
        cp.wait_send()


def shards(
    queries,
    fresh_entries,
    cache_blocks,
    lengths,
    migration,
    residual,
    out_weight,
    norm_gain,
    routes,
    route_gates,
    w_gate,
    w_up,
    w_down,
):
    vmem = pl.BlockSpec(memory_space=pltpu.VMEM)
    smem = pl.BlockSpec(memory_space=pltpu.SMEM)
    hbm = pl.BlockSpec(memory_space=pl.ANY)
    block = (2 * TOK, HALF)

    def buf(*shape, dtype=BF16):
        return pltpu.VMEM(shape, dtype)

    return pl.pallas_call(
        kernel,
        out_shape=(
            jax.ShapeDtypeStruct((2, REQS, PART), BF16),
            jax.ShapeDtypeStruct((8, ROWS, 512), BF16),
        ),
        in_specs=[vmem, vmem, hbm, smem, smem, vmem, hbm, vmem, vmem, vmem, hbm, hbm, hbm],
        out_specs=(vmem, hbm),
        scratch_shapes=[
            buf(REQS, BLOCKS, ROWS, 512),
            buf(PART, D),
            buf(D, 512),
            buf(256, D),
            buf(8, ROWS, 512),
            buf(TOK, D, dtype=F32),
            buf(QH * TOK, HD),
            buf(2, 2, TOK, HD, dtype=F32),
            buf(TOK, PART, dtype=F32),
            buf(N_P, OWN * TOK + 16, HD),
            buf(N_P, OWN * TOK + 16, HD),
            buf(N_P, *block),
            buf(N_P, *block),
            buf(*block, dtype=F32),
            buf(2, NX, NZL, TOK, 128, dtype=F32),
            buf(2, 4, 4, N_Z, *block),
            buf(ALL, 512, dtype=F32),
            buf(ALL, 128, dtype=F32),
            buf(ALL, 256),
            buf(2, 4, 4, N_Z, *block),
            buf(4, 4, N_Z, *block),
            buf(4, 4, N_Z, *block),
            buf(6, 2, N_Z, *block),
            buf(2, 2, N_Z, *block),
            buf(4, N_Z, *block),
            buf(6, N_Z // 2, *block),
            buf(2, N_Z // 2, *block),
            buf(N_Z, *block, dtype=F32),
            buf(N_Z, *block),
            buf(N_Z, *block),
            buf(TOK, PART, dtype=F32),
            pltpu.SemaphoreType.DMA((16,)),
            pltpu.SemaphoreType.DMA((N_SEMS,)),
            pltpu.SemaphoreType.DMA((N_SEMS,)),
        ],
        compiler_params=pltpu.CompilerParams(
            collective_id=0, has_side_effects=True, vmem_limit_bytes=48 * MIB
        ),
        cost_estimate=pl.CostEstimate(
            flops=2_000_000_000, bytes_accessed=13 * MIB, transcendentals=200_000
        ),
    )(
        queries,
        fresh_entries,
        cache_blocks,
        lengths,
        migration,
        residual,
        out_weight,
        norm_gain.reshape(1, D),
        routes,
        route_gates,
        w_gate,
        w_up,
        w_down,
    )


def solution(mesh):
    in_specs = (
        P(None, "dp", None),
        P(None, "dp", None),
        P("dp", None, "expert", None),
        P("dp"),
        P("dp", None),
        P(None, "dp", None),
        P("expert", None),
        P(),
        P(None, "dp", None),
        P(None, "dp", None),
        P("dp", None, "expert"),
        P("dp", None, "expert"),
        P("dp", "expert", None),
    )
    out_specs = (P(None, "dp", "expert"), P("dp", "expert", None))
    return jax.shard_map(shards, mesh=mesh, in_specs=in_specs, out_specs=out_specs, check_vma=False)
```

time: 2200 us -> 87.6 us (0.04)
  waiting for transfers between devices: 2100 us -> 0 us
  Pallas kernels: 0 us -> 76.1 us
  blocking collectives: 34.1 us -> 0 us
    reduce_scatter x2 -> x0, waiting for transfers between devices: 1420 us -> none  [the longest x1 1340 us: shards(): mixed = lax.psum_scatter(mixed, ('dp', 'expert'), scatter_dimension=0)]
    all_gather x1 -> x0, waiting for transfers between devices: 656 us -> none  [shards(): gathered = lax.all_gather(hidden.astype(jnp.bfloat16), ('dp', 'expert'))]
    pallas_call x0 -> x1, Pallas kernels: none -> 76.1 us  [shards(): pl.pallas_call(kernel, out_shape=(jax.ShapeDtypeStruct((2, REQS, PART), B...]
    all_gather x1 -> x0, blocking collectives: 34.1 us -> none  [shards(): coef_all = lax.all_gather(coef, 'dp').reshape(n_dp * tokens, EXPERTS)]
  transfers between devices with their start and end apart: 6 -> 0, of which waited for: 6 -> 0; matrix products, arithmetic and copies ran while one was open for 0% -> 0% of each run, Pallas kernels for 0% -> 0%
where the time goes in v2:
time: 87.6 us; the launch traced here: 87.1 us
  Pallas kernels  76.1 us (87%)
  local copies, waits for them, and re-layouts  10.3 us (12%)
    pallas_call x1, Pallas kernels, shards(): pl.pallas_call(kernel, out_shape=(jax.ShapeDtypeStruct((2, REQS, PART), B...  76.1 us
    unnamed x21, local copies, waits for them, and re-layouts  10.3 us

profile of v2, /device:TPU:2, one launch (start us, length us, event | category | flops | bytes accessed | tf_op | source)
XLA Modules:
  0.0 87.1 jit_solution(14391378582339494080)
XLA Ops:
  0.6 0.8 copy.15.mig_ref
  1.4 0.0 copy-start
  1.4 1.6 %copy-done = bf16[4,32,16,512]{3,2,1,0:T(8,128)(2,1)S(1)} copy-done((bf16[4,32,16,512]{3,2,1,0:T(8,128)(2,1)S(1)}, bf16[4,32,16,512]{3,2,1,0:T(8,128)(2,1)}, u32[]{:S(2)}) %copy-start) | copy-done | bytes 2097176
  3.0 0.0 copy-start.1
  3.0 1.6 %copy-done.1 = bf16[2,4096,128]{2,1,0:T(8,128)(2,1)S(1)} copy-done((bf16[2,4096,128]{2,1,0:T(8,128)(2,1)S(1)}, bf16[2,4096,128]{2,1,0:T(8,128)(2,1)}, u32[]{:S(2)}) %copy-start.1) | copy-done | bytes 2097176
  4.6 0.0 copy-start.2
  4.6 0.8 copy-done.2
  5.4 0.0 copy-start.3
  5.4 0.8 copy-done.3
  6.2 0.0 copy-start.4
  6.2 0.7 copy-done.4
  7.0 0.0 copy-start.5
  7.0 0.7 copy-done.5
  7.7 0.0 copy-start.6
  7.7 0.7 copy-done.6
  8.3 0.0 copy-start.7
  8.4 0.7 copy-done.7
  9.0 0.0 copy-start.8
  9.0 0.7 copy-done.8
  9.7 76.1 %shard_map.140 = (bf16[2,4,512]{2,1,0:T(4,128)(2,1)S(1)}, bf16[8,16,512]{2,1,0:T(8,128)(2,1)S(1)}) custom-call(bf16[2,4,4096]{2,1,0:T(4,128)(2,1)S(1)} %copy-done.2, bf16[2,4,512]{2,1,0:T(4,128)(2,1)S(1)} %copy-done.5, bf16[4,32,16,512]{3,2,1,0:T(8,128)(2,1)S(1)} %copy-done, s32[4]{0:T(128)S(1)} %copy-done.8, s32[8,2]{1,0:T(8,128)S(1)} %copy.15.mig_ref, ...), custom_call_target="tpu_custom_call" | custom-call | flops 2000000000 | bytes 13631488 | tf_op jit(solution)/shard_map/pallas_call | solution.py:495
  85.8 0.6 copy.18
  86.4 0.7 copy.19
Async XLA Ops:
  1.4 1.6 %copy-start = (bf16[4,32,16,512]{3,2,1,0:T(8,128)(2,1)S(1)}, bf16[4,32,16,512]{3,2,1,0:T(8,128)(2,1)}, u32[]{:S(2)}) copy-start(bf16[4,32,16,512]{3,2,1,0:T(8,128)(2,1)} %cache_ref.1) | copy-start | bytes 6291460
  3.0 1.6 %copy-start.1 = (bf16[2,4096,128]{2,1,0:T(8,128)(2,1)S(1)}, bf16[2,4096,128]{2,1,0:T(8,128)(2,1)}, u32[]{:S(2)}) copy-start(bf16[2,4096,128]{2,1,0:T(8,128)(2,1)} %wg_ref.1) | copy-start | bytes 6291460
  4.6 0.8 copy-start.2
  5.4 0.8 copy-start.3
  6.2 0.7 copy-start.4
  7.0 0.7 copy-start.5
  7.7 0.7 copy-start.6
  8.3 0.7 copy-start.7
  9.0 0.7 copy-start.8

commit v3 on v2

v3 whole, which is shorter than its diff:
```python
import functools
import math

import jax
import jax.numpy as jnp
from jax import lax
from jax.experimental import pallas as pl
from jax.experimental.pallas import tpu as pltpu
from jax.sharding import PartitionSpec as P

MESH = pl.DeviceIdType.MESH
HD = 128
QH = 32
KVH = 2
TOPK = 8
BLOCKS = 32
NX, NZL, NY, NZH = 4, 4, 4, 2
N_P = NY * NZH
N_Z = NZH * NZL
N_DP = NX * NZL * 2
REQS = 4
TOK = 2 * REQS
D = 4096
PART = D // N_P
HALF = PART // 2
PAIR = 2 * PART
FAR_Z = (4, 3, 5, 2, 6, 1, 7)
FAR_P = (3, 5, 1, 7, 4, 2, 6)
ROWS = 16
POSN = BLOCKS * ROWS
OWN = QH // N_P
ALL = N_DP * TOK
F32 = jnp.float32
BF16 = jnp.bfloat16
NEG = -1e30
N_SEMS = 88
MIB = 1024 * 1024


def kernel(
    q_ref,
    fresh_ref,
    cache_ref,
    len_ref,
    mig_ref,
    res_ref,
    ow_ref,
    gain_ref,
    routes_ref,
    gates_ref,
    wg_ref,
    wu_ref,
    wd_ref,
    out_ref,
    guest_ref,
    q_v,
    fresh_v,
    len_v,
    mig_s,
    res_v,
    gain_v,
    routes_v,
    gates_v,
    cache_v,
    ow_v,
    wgu_v,
    wd_v,
    picked_v,
    q_s,
    q_b,
    f_s,
    r_s,
    a_send,
    a_recv,
    b_send,
    b_recv,
    zr,
    hid,
    rt,
    g_buf,
    rows_v,
    ssq,
    act,
    p_buf,
    s_buf,
    m_buf,
    a_in,
    n_buf,
    b_in,
    n2_buf,
    z_send,
    z_recv,
    o_s,
    load_sem,
    send_sem,
    recv_sem,
):
    me = lax.axis_index("dp")
    p = lax.axis_index("expert")
    core = lax.rem(me, 2)
    zlo = lax.rem(lax.div(me, 2), NZL)
    x = lax.div(me, 2 * NZL)
    y = lax.div(p, NZH)
    zhi = lax.rem(p, NZH)
    z = zhi * NZL + zlo

    def place(x_, y_, zlo_, zhi_, core_):
        return ((x_ * NZL + zlo_) * 2 + core_, y_ * NZH + zhi_)

    def at_p(k):
        return (me, lax.rem(p + k, N_P))

    def at_y(k):
        return place(x, lax.rem(y + k, NY), zlo, zhi, core)

    def at_z(k):
        t = lax.rem(z + k, N_Z)
        return place(x, y, lax.rem(t, NZL), lax.div(t, NZL), core)

    def at_x(k):
        return place(lax.rem(x + k, NX), y, zlo, zhi, core)

    def at_zlo(k):
        return place(x, y, lax.rem(zlo + k, NZL), zhi, core)

    def at_a(k):
        return place(lax.rem(x + (1 - core) * k, NX), lax.rem(y + core * k, NY), zlo, zhi, core)

    def at_b(k):
        return place(lax.rem(x + core * k, NX), lax.rem(y + (1 - core) * k, NY), zlo, zhi, core)

    sibling = place(x, y, zlo, zhi, 1 - core)
    ia = (1 - core) * x + core * y
    ib = core * x + (1 - core) * y
    sib_ib = ia

    loads = []

    def load(src, dst):
        cp = pltpu.make_async_copy(src, dst, load_sem.at[len(loads)])
        cp.start()
        loads.append(cp)
        return cp

    small_cp = [load(routes_ref, routes_v), load(gates_ref, gates_v), load(q_ref, q_v)]
    len_cp = load(len_ref, len_v)
    mig_cp = load(mig_ref, mig_s)
    cache_cp = [load(cache_ref.at[r], cache_v.at[r]) for r in range(REQS)]
    fresh_cp = load(fresh_ref, fresh_v)
    res_cp = load(res_ref, res_v)
    gain_cp = load(gain_ref, gain_v)
    ow_cp = load(ow_ref, ow_v)
    w_cp = []
    for j in range(2):
        w_cp.append(load(wg_ref.at[j], wgu_v.at[:, pl.ds(256 * j, 128)]))
        w_cp.append(load(wu_ref.at[j], wgu_v.at[:, pl.ds(256 * j + 128, 128)]))
    wd_cp = [load(wd_ref.at[j], wd_v.at[pl.ds(128 * j, 128)]) for j in range(2)]

    barrier = pltpu.get_barrier_semaphore()
    peers = [at_p(k) for k in range(1, N_P)]
    peers += [at_z(k) for k in range(1, N_Z) if k != NZL]
    peers += [at_x(k) for k in range(1, NX)]
    peers += [sibling]
    for peer in peers:
        pl.semaphore_signal(barrier, inc=1, device_id=peer, device_id_type=MESH)

    sent = []

    def send(src, dst, peer):
        k = len(sent)
        cp = pltpu.make_async_remote_copy(
            src_ref=src,
            dst_ref=dst,
            send_sem=send_sem.at[k],
            recv_sem=recv_sem.at[k],
            device_id=peer,
            device_id_type=MESH,
        )
        cp.start()
        sent.append(cp)
        return cp

    for cp in small_cp:
        cp.wait()

    lane = lax.broadcasted_iota(jnp.int32, (REQS, 128), 1)
    for s in range(2):
        ids = routes_v[s]
        vals = gates_v[s]
        coef = jnp.zeros((REQS, 128), F32)
        for k in range(TOPK):
            coef = coef + jnp.where(lane == ids[:, k : k + 1], vals[:, k : k + 1], 0.0)
        rt[core, x, zlo, pl.ds(REQS * s, REQS), :] = coef

    for s in range(2):
        q_s[pl.ds(REQS * s, REQS), :] = q_v[s].astype(F32)
    q_b[...] = jnp.concatenate(
        [q_s[:, h * HD : (h + 1) * HD] for h in range(QH)], axis=0
    ).astype(BF16)

    mig_cp.wait()
    len_cp.wait()
    for cp in cache_cp:
        cp.wait()
    for m in range(8):
        picked_v[m] = cache_v[mig_s[0, m], mig_s[1, m]]

    scale = 1.0 / math.sqrt(HD)
    col = lax.broadcasted_iota(jnp.int32, (TOK, POSN), 1)
    row = lax.rem(lax.broadcasted_iota(jnp.int32, (TOK, POSN), 0), REQS)
    position = lax.div(col, ROWS) * (ROWS * N_P) + p * ROWS + lax.rem(col, ROWS)
    limit = jnp.full((TOK, POSN), 0, jnp.int32)
    for r in range(REQS):
        limit = jnp.where(row == r, len_v[0:1, r : r + 1], limit)
    valid = position < limit
    hk = QH // KVH * TOK
    rid = lax.rem(lax.broadcasted_iota(jnp.int32, (hk, POSN), 0), REQS)
    rid_o = lax.rem(lax.broadcasted_iota(jnp.int32, (hk, HD), 0), REQS)
    sub = lax.broadcasted_iota(jnp.int32, (OWN * TOK, 128), 0)
    lan = lax.broadcasted_iota(jnp.int32, (OWN * TOK, 128), 1)
    for k in range(KVH):
        qk = q_b[k * hk : (k + 1) * hk]
        scores = None
        for r in range(REQS):
            keys = cache_v[r, :, :, k * HD : (k + 1) * HD].reshape(POSN, HD)
            part = lax.dot_general(
                qk, keys, (((1,), (1,)), ((), ())), preferred_element_type=F32
            )
            scores = part if r == 0 else jnp.where(rid == r, part, scores)
        scores = scores.reshape(hk // TOK, TOK, POSN)
        scores = jnp.where(valid[None], scores * scale, NEG)
        peak = jnp.max(scores, -1, keepdims=True).astype(BF16).astype(F32)
        weights = jnp.exp(scores - peak)
        total = jnp.sum(weights, -1, keepdims=True)
        weights = weights.reshape(hk, POSN).astype(BF16)
        state = None
        for r in range(REQS):
            vals = cache_v[r, :, :, (KVH + k) * HD : (KVH + k + 1) * HD].reshape(POSN, HD)
            part = jnp.dot(weights, vals, preferred_element_type=F32)
            state = part if r == 0 else jnp.where(rid_o == r, part, state)
        peak = peak.reshape(hk, 1)
        total = total.reshape(hk, 1)
        total_hi = total.astype(BF16).astype(F32)
        total_lo = total - total_hi
        n_rows = OWN * TOK
        for i in range(hk // n_rows):
            dest = k * (hk // n_rows) + i
            rows = slice(i * n_rows, (i + 1) * n_rows)
            a_send[dest, 0:n_rows, :] = state[rows].astype(BF16)
            stat = jnp.where(lan == sub, peak[rows], 0.0)
            stat = jnp.where(lan == sub + n_rows, total_hi[rows], stat)
            stat = jnp.where(lan == sub + 2 * n_rows, total_lo[rows], stat)
            stat = jnp.sum(stat, axis=0, keepdims=True)
            a_send[dest, n_rows : n_rows + 16, :] = jnp.broadcast_to(stat, (16, 128)).astype(BF16)

    pl.semaphore_wait(barrier, len(peers))

    a_cp = []
    for k in FAR_P:
        a_cp.append(send(a_send.at[lax.rem(p + k, N_P)], a_recv.at[k], at_p(k)))
    rt_cp = [
        send(rt.at[core, x, zlo], rt.at[core, x, zlo], at_zlo(k)) for k in range(1, NZL)
    ]
    guest_cp = send(picked_v, guest_ref, at_x(2))
    a_recv[0] = a_send[p]

    fresh_cp.wait()
    kv = lax.div(p, N_P // KVH)
    for n in range(2):
        for j in range(2):
            new = fresh_v[
                n, :, pl.ds(pl.multiple_of((j * KVH + kv) * HD, HD), HD)
            ].astype(F32)
            f_s[n, j, 0:REQS, :] = new
            f_s[n, j, REQS:TOK, :] = new
    q_own = q_s[:, pl.ds(pl.multiple_of(p * PART, PART), PART)]
    q_own = jnp.stack([q_own[:, i * HD : (i + 1) * HD] for i in range(OWN)], axis=0)
    f_scores = [
        jnp.sum(q_own * f_s[n, 0][None], -1, keepdims=True) * scale for n in range(2)
    ]
    step_row = lax.broadcasted_iota(jnp.int32, (OWN, TOK, 1), 1)
    f_scores[1] = jnp.where(step_row >= REQS, f_scores[1], NEG)

    for cp in a_cp:
        cp.wait_recv()
    n_rows = OWN * TOK

    def to_row(v):
        return jnp.sum(jnp.where(lan == sub, v, 0.0), axis=0, keepdims=True)

    def to_col(v):
        return jnp.sum(jnp.where(lan == sub, v, 0.0), axis=1, keepdims=True)

    stat = jnp.concatenate(
        [a_recv[k, n_rows : n_rows + 16, :].astype(F32)[0:1] for k in range(N_P)], axis=0
    )
    totals = pltpu.roll(stat, 128 - n_rows, 1) + pltpu.roll(stat, 128 - 2 * n_rows, 1)
    f_scores = [to_row(f.reshape(n_rows, 1)) for f in f_scores]
    top = jnp.maximum(jnp.max(stat, axis=0, keepdims=True), jnp.maximum(f_scores[0], f_scores[1]))
    used = lan[0:1] < n_rows
    w_dev = jnp.exp(jnp.where(used, stat - top, NEG))
    w_new = [jnp.exp(jnp.where(used, f - top, NEG)) for f in f_scores]
    denom = jnp.sum(w_dev * totals, axis=0, keepdims=True) + w_new[0] + w_new[1]
    denom = 1.0 / jnp.where(used, denom, 1.0)
    w_dev = w_dev * denom
    numer = jnp.zeros((n_rows, HD), F32)
    for n in range(2):
        vals = jnp.broadcast_to(f_s[n, 1][None], (OWN, TOK, HD)).reshape(n_rows, HD)
        numer = numer + to_col(w_new[n] * denom) * vals
    for k in range(N_P):
        numer = numer + to_col(w_dev[k : k + 1]) * a_recv[k, 0:n_rows, :].astype(F32)
    attention = numer.reshape(OWN, TOK, HD)
    attention = jnp.concatenate([attention[i] for i in range(OWN)], axis=1).astype(BF16)

    for cp in rt_cp:
        cp.wait_recv()
    rt_cp = [send(rt.at[core, x], rt.at[core, x], at_x(k)) for k in range(1, NX)]

    def packed(v):
        half = v.shape[1] // 2
        return jnp.concatenate([v[:, 0:half], v[:, half:]], axis=0)

    def unpacked(v):
        return jnp.concatenate([v[0:TOK], v[TOK : 2 * TOK]], axis=1)

    res_cp.wait()
    at = pl.ds(pl.multiple_of(y * PAIR, PAIR), PAIR)
    for s in range(2):
        r_s[pl.ds(REQS * s, REQS), :] = res_v[s, :, at].astype(F32)
    ow_cp.wait()
    b_cp = []
    for k in (2, 1, 3, 0):
        yy = lax.rem(y + k, NY)
        term = jnp.dot(
            attention,
            ow_v[:, pl.ds(pl.multiple_of(yy * PAIR, PAIR), PAIR)],
            preferred_element_type=F32,
        )
        if k != 0:
            b_send[k] = packed(term).astype(BF16)
            b_cp.append(send(b_send.at[k], b_recv.at[k], at_y(k)))
    hidden = packed(jnp.where(zhi == 0, r_s[...], 0.0) + term)
    for k, cp in zip((2, 1, 3), b_cp):
        cp.wait_recv()
        hidden = hidden + b_recv[k].astype(F32)
    zr[z] = hidden.astype(BF16)

    z_cp = [send(zr.at[z], zr.at[z], at_z(k)) for k in FAR_Z]
    for cp in rt_cp:
        cp.wait_recv()
    rt_cp = [send(rt.at[core], rt.at[core], sibling)]
    for cp in z_cp:
        cp.wait_recv()
    for t in range(NZL):
        hidden = zr[t].astype(F32) + zr[NZL + t].astype(F32)
        g_buf[core, ia, ib, t] = hidden.astype(BF16)
    hidden = zr[zlo].astype(F32) + zr[NZL + zlo].astype(F32)
    hid[0] = hidden[0:TOK]
    hid[1] = hidden[TOK : 2 * TOK]

    def to_ring(jb):
        piece = g_buf.at[core, ia, jb]
        return [send(piece, piece, at_a(k)) for k in (2, 1, 3)]

    mine = g_buf.at[core, ia, ib]
    b_cp = {k: send(mine, mine, at_b(k)) for k in (2, 1, 3)}
    a_cp = [to_ring(ib)]
    for k in (1, 3, 2):
        b_cp[k].wait_recv()
        a_cp.append(to_ring(lax.rem(ib + 4 - k, 4)))

    gain_cp.wait()
    ssq[...] = jnp.zeros_like(ssq)

    def prepare(plane, jb):
        def step(ja, _):
            xx = (1 - plane) * ja + plane * jb
            yy = plane * ja + (1 - plane) * jb
            blocks = g_buf[plane, ja, jb].astype(F32)
            rows = jnp.concatenate(
                [
                    blocks[:, 0:TOK].reshape(NZL * TOK, PART),
                    blocks[:, TOK : 2 * TOK].reshape(NZL * TOK, PART),
                ],
                axis=1,
            )
            sq = rows * rows
            while sq.shape[1] > 128:
                half = sq.shape[1] // 2
                sq = sq[:, 0:half] + sq[:, half:]
            at_row = pl.ds(pl.multiple_of(plane * (ALL // 2) + xx * (NZL * TOK), NZL * TOK), NZL * TOK)
            at_col = pl.ds(pl.multiple_of(yy * PAIR, PAIR), PAIR)
            ssq[at_row, :] += sq
            rows_v[at_row, at_col] = (rows * gain_v[:, at_col]).astype(BF16)
            return 0

        lax.fori_loop(0, 4, step, 0)

    def across(ja, jb):
        piece = g_buf.at[core, ja, jb]
        return send(piece, piece, sibling)

    order = (0, 1, 3, 2)
    c_cp = [[across(ia, lax.rem(ib + 4 - k, 4))] for k in order]
    for i, k in enumerate(order):
        jb = lax.rem(ib + 4 - k, 4)
        for ka, cp in zip((2, 1, 3), a_cp[i]):
            cp.wait_recv()
            c_cp[i].append(across(lax.rem(ia + 4 - ka, 4), jb))
        prepare(core, jb)
        if i > 0:
            for cp in c_cp[i - 1]:
                cp.wait_recv()
            prepare(1 - core, lax.rem(sib_ib + 4 - order[i - 1], 4))
    for cp in c_cp[3]:
        cp.wait_recv()
    prepare(1 - core, lax.rem(sib_ib + 4 - order[3], 4))
    for cp in rt_cp:
        cp.wait_recv()

    for cp in w_cp:
        cp.wait()
    spread = jnp.sum(ssq[...], -1, keepdims=True) * (1.0 / D)
    norm = lax.rsqrt(spread + 1e-06)
    coefs = rt[...].reshape(ALL, 128)
    lane = lax.broadcasted_iota(jnp.int32, (ALL, 128), 1)
    for j in range(2):
        coef = jnp.sum(jnp.where(lane == 2 * me + j, coefs, 0.0), -1, keepdims=True)
        both = jnp.dot(
            rows_v[...], wgu_v[:, 256 * j : 256 * j + 256], preferred_element_type=F32
        )
        gate = both[:, 0:128] * norm
        up = both[:, 128:256] * norm
        inner = gate / (1.0 + jnp.exp(-gate)) * up
        act[:, 128 * j : 128 * j + 128] = (inner * coef).astype(BF16)

    for cp in wd_cp:
        cp.wait()

    def down_step(yy, _):
        at = pl.ds(pl.multiple_of(yy * PAIR, PAIR), PAIR)
        made = jnp.dot(act[...], wd_v[:, at], preferred_element_type=F32)
        made = made.reshape(2, NX * NZL, TOK, PAIR)
        made = jnp.concatenate([made[..., 0:PART], made[..., PART:PAIR]], axis=2)
        made = made.astype(BF16).reshape(2, NX, NZL, 2 * TOK, PART)
        p_buf[0, :, yy] = made[0]
        p_buf[1, yy] = made[1]
        return 0

    lax.fori_loop(0, NY, down_step, 0)

    order = (2, 1, 3, 0)
    c_cp = []
    for k in order:
        jb = lax.rem(sib_ib + k, 4)
        c_cp.append(send(p_buf.at[1 - core, :, jb], s_buf.at[:, jb], sibling))
    a_cp = []
    for i, k in enumerate(order):
        c_cp[i].wait_recv()
        jb = lax.rem(ib + k, 4)
        m_buf[:, jb] = (p_buf[core, :, jb].astype(F32) + s_buf[:, jb].astype(F32)).astype(BF16)
        a_cp.append(
            [
                send(m_buf.at[lax.rem(ia + ka, 4), jb], a_in.at[i, ka], at_a(ka))
                for ka in (2, 1, 3)
            ]
        )
    b_cp = []
    for i, k in enumerate(order):
        for cp in a_cp[i]:
            cp.wait_recv()
        jb = lax.rem(ib + k, 4)
        total = m_buf[ia, jb].astype(F32)
        for ka in range(1, 4):
            total = total + a_in[i, ka].astype(F32)
        if k != 0:
            n_buf[k] = total.astype(BF16)
            b_cp.append(send(n_buf.at[k], b_in.at[k], at_b(k)))
    for k, cp in zip(order, b_cp):
        cp.wait_recv()
        total = total + b_in[k].astype(F32)
    for t in range(NZL):
        n2_buf[t] = packed(total[t, 0:TOK])
        n2_buf[NZL + t] = packed(total[t, TOK : 2 * TOK])
    z_send[...] = n2_buf[...].astype(BF16)
    z_cp = [send(z_send.at[lax.rem(z + k, N_Z)], z_recv.at[k], at_z(k)) for k in FAR_Z]
    result = packed(hid[zhi]) + n2_buf[z]
    for k, cp in zip(FAR_Z, z_cp):
        cp.wait_recv()
        result = result + z_recv[k].astype(F32)
    o_s[...] = unpacked(result)
    for s in range(2):
        out_ref[s] = o_s[REQS * s : REQS * (s + 1), :].astype(BF16)
    guest_cp.wait_recv()
    for cp in sent:
        cp.wait_send()


def finish_kernel(a_ref, b_ref, a_out, b_out, a_v, b_v, sem):
    pairs = [(a_ref, a_v), (b_ref, b_v), (a_v, a_out), (b_v, b_out)]
    copies = [pltpu.make_async_copy(*pair, sem.at[i]) for i, pair in enumerate(pairs)]
    copies[0].start()
    copies[1].start()
    for i in range(2):
        copies[i].wait()
        copies[i + 2].start()
    for i in range(2):
        copies[i + 2].wait()


def shards(
    queries,
    fresh_entries,
    cache_blocks,
    lengths,
    migration,
    residual,
    out_weight,
    norm_gain,
    routes,
    route_gates,
    w_gate,
    w_up,
    w_down,
):
    vmem = pl.BlockSpec(memory_space=pltpu.VMEM)
    hbm = pl.BlockSpec(memory_space=pltpu.HBM)
    pair = (2 * TOK, PART)
    block = (2 * TOK, HALF)

    def buf(*shape, dtype=BF16):
        return pltpu.VMEM(shape, dtype)

    shapes = (
        jax.ShapeDtypeStruct((2, REQS, PART), BF16),
        jax.ShapeDtypeStruct((8, ROWS, 512), BF16),
    )
    made = pl.pallas_call(
        kernel,
        out_shape=shapes,
        in_specs=[hbm] * 13,
        out_specs=(vmem, hbm),
        scratch_shapes=[
            buf(2, REQS, D),
            buf(2, REQS, 512),
            buf(1, REQS, dtype=jnp.int32),
            pltpu.SMEM((2, 8), jnp.int32),
            buf(2, REQS, D),
            buf(1, D, dtype=F32),
            buf(2, REQS, TOPK, dtype=jnp.int32),
            buf(2, REQS, TOPK, dtype=F32),
            buf(REQS, BLOCKS, ROWS, 512),
            buf(PART, D),
            buf(D, 512),
            buf(256, D),
            buf(8, ROWS, 512),
            buf(TOK, D, dtype=F32),
            buf(QH * TOK, HD),
            buf(2, 2, TOK, HD, dtype=F32),
            buf(TOK, PAIR, dtype=F32),
            buf(N_P, OWN * TOK + 16, HD),
            buf(N_P, OWN * TOK + 16, HD),
            buf(NY, *pair),
            buf(NY, *pair),
            buf(N_Z, *pair),
            buf(2, TOK, PART, dtype=F32),
            buf(2, NX, NZL, TOK, 128, dtype=F32),
            buf(2, 4, 4, NZL, *pair),
            buf(ALL, D),
            buf(ALL, 128, dtype=F32),
            buf(ALL, 256),
            buf(2, 4, 4, NZL, *pair),
            buf(4, 4, NZL, *pair),
            buf(4, 4, NZL, *pair),
            buf(4, 4, NZL, *pair),
            buf(4, NZL, *pair),
            buf(4, NZL, *pair),
            buf(N_Z, *block, dtype=F32),
            buf(N_Z, *block),
            buf(N_Z, *block),
            buf(TOK, PART, dtype=F32),
            pltpu.SemaphoreType.DMA((24,)),
            pltpu.SemaphoreType.DMA((N_SEMS,)),
            pltpu.SemaphoreType.DMA((N_SEMS,)),
        ],
        compiler_params=pltpu.CompilerParams(
            collective_id=0, has_side_effects=True, vmem_limit_bytes=60 * MIB
        ),
        cost_estimate=pl.CostEstimate(
            flops=2_000_000_000, bytes_accessed=13 * MIB, transcendentals=200_000
        ),
    )(
        queries,
        fresh_entries,
        cache_blocks,
        lengths.reshape(1, REQS),
        migration.T,
        residual,
        out_weight,
        norm_gain.reshape(1, D),
        routes,
        route_gates,
        w_gate,
        w_up,
        w_down,
    )
    return pl.pallas_call(
        finish_kernel,
        out_shape=shapes,
        in_specs=[hbm] * 2,
        out_specs=(hbm, hbm),
        scratch_shapes=[
            buf(2, REQS, PART),
            buf(8, ROWS, 512),
            pltpu.SemaphoreType.DMA((4,)),
        ],
        compiler_params=pltpu.CompilerParams(vmem_limit_bytes=60 * MIB),
    )(*made)


def solution(mesh):
    in_specs = (
        P(None, "dp", None),
        P(None, "dp", None),
        P("dp", None, "expert", None),
        P("dp"),
        P("dp", None),
        P(None, "dp", None),
        P("expert", None),
        P(),
        P(None, "dp", None),
        P(None, "dp", None),
        P("dp", None, "expert"),
        P("dp", None, "expert"),
        P("dp", "expert", None),
    )
    out_specs = (P(None, "dp", "expert"), P("dp", "expert", None))
    return jax.shard_map(shards, mesh=mesh, in_specs=in_specs, out_specs=out_specs, check_vma=False)
```

time: 87.6 us -> 64.5 us (0.74)
  Pallas kernels: 76.1 us -> 63.3 us
  local copies, waits for them, and re-layouts: 10.3 us -> 0 us
    pallas_call x1 -> x2, Pallas kernels: 76.1 us -> 63.3 us  [the longest x1 61.7 us: shards(): pl.pallas_call(kernel, out_shape=shapes, in_specs=[hbm] * 13, out_specs=(...]
    unnamed x21 -> x0, local copies, waits for them, and re-layouts: 10.3 us -> none
where the time goes in v3:
time: 64.5 us; the launch traced here: 64 us
  Pallas kernels  63.3 us (98%)
    pallas_call x1, Pallas kernels, shards(): pl.pallas_call(kernel, out_shape=shapes, in_specs=[hbm] * 13, out_specs=(...  61.7 us
    pallas_call x1, Pallas kernels, shards(): pl.pallas_call(finish_kernel, out_shape=shapes, in_specs=[hbm] * 2, out_s...  1.61 us

profile of v3, /device:TPU:2, one launch (start us, length us, event | category | flops | bytes accessed | tf_op | source)
XLA Modules:
  0.0 64.0 jit_solution(15212079796835112240)
XLA Ops:
  0.6 61.7 %shard_map.140 = (bf16[2,4,512]{2,1,0:T(4,128)(2,1)}, bf16[8,16,512]{2,1,0:T(8,128)(2,1)}) custom-call(bf16[2,4,4096]{2,1,0:T(4,128)(2,1)} %q_ref.1, bf16[2,4,512]{2,1,0:T(4,128)(2,1)} %fresh_ref.1, bf16[4,32,16,512]{3,2,1,0:T(8,128)(2,1)} %cache_ref.1, s32[1,4]{1,0:T(1,128)} %bitcast.5, s32[2,8]{1,0:T(2,128)} %bitcast.4, bf16[2,4,4096]{2,1,0:T(4,128)(2,1)} %res_ref.1, ...), custom_call_target="tpu_custom_call" | custom-call | flops 2000000000 | bytes 13631488 | tf_op jit(solution)/shard_map/pallas_call | solution.py:538
  62.4 1.6 %shard_map.141 = (bf16[2,4,512]{2,1,0:T(4,128)(2,1)}, bf16[8,16,512]{2,1,0:T(8,128)(2,1)}) custom-call(bf16[2,4,512]{2,1,0:T(4,128)(2,1)} %get-tuple-element.4.a_ref, bf16[8,16,512]{2,1,0:T(8,128)(2,1)} %get-tuple-element.5.b_ref), custom_call_target="tpu_custom_call" | custom-call | tf_op jit(solution)/shard_map/pallas_call | solution.py:607

commit v4 on v3

--- a/solution.py
+++ b/solution.py
@@ -24,7 +24,9 @@
 PART = D // N_P
 HALF = PART // 2
 PAIR = 2 * PART
-FAR_Z = (4, 3, 5, 2, 6, 1, 7)
+Z_LABELS = (5, 6, 2, 1, 4, 3, 7)
+OFFSETS = ((2, 1), (3, 0))
+SLOT = {2: 0, 1: 1, 3: 2, 0: 3}
 FAR_P = (3, 5, 1, 7, 4, 2, 6)
 ROWS = 16
 POSN = BLOCKS * ROWS
@@ -33,7 +35,7 @@
 F32 = jnp.float32
 BF16 = jnp.bfloat16
 NEG = -1e30
-N_SEMS = 88
+N_SEMS = 180
 MIB = 1024 * 1024
 
 
@@ -86,10 +88,9 @@
     m_buf,
     a_in,
     n_buf,
-    b_in,
-    n2_buf,
-    z_send,
-    z_recv,
+    t_buf,
+    e_send,
+    e_recv,
     o_s,
     load_sem,
     send_sem,
@@ -129,10 +130,30 @@
     def at_b(k):
         return place(lax.rem(x + core * k, NX), lax.rem(y + (1 - core) * k, NY), zlo, zhi, core)
 
+    def at_bz(kb, kz):
+        t = lax.rem(z + kz, N_Z)
+        return place(
+            lax.rem(x + core * kb, NX),
+            lax.rem(y + (1 - core) * kb, NY),
+            lax.rem(t, NZL),
+            lax.div(t, NZL),
+            core,
+        )
+
     sibling = place(x, y, zlo, zhi, 1 - core)
     ia = (1 - core) * x + core * y
     ib = core * x + (1 - core) * y
     sib_ib = ia
+    sib_ia = ib
+
+    barrier = pltpu.get_barrier_semaphore()
+    peers = [at_p(k) for k in range(1, N_P)]
+    peers += [at_z(k) for k in range(1, N_Z) if k != NZL]
+    peers += [at_x(k) for k in range(1, NX)]
+    peers += [at_bz(kb, kz) for kb in range(1, 4) for kz in range(1, N_Z)]
+    peers += [sibling]
+    for peer in peers:
+        pl.semaphore_signal(barrier, inc=1, device_id=peer, device_id_type=MESH)
 
     loads = []
 
@@ -149,21 +170,6 @@
     fresh_cp = load(fresh_ref, fresh_v)
     res_cp = load(res_ref, res_v)
     gain_cp = load(gain_ref, gain_v)
-    ow_cp = load(ow_ref, ow_v)
-    w_cp = []
-    for j in range(2):
-        w_cp.append(load(wg_ref.at[j], wgu_v.at[:, pl.ds(256 * j, 128)]))
-        w_cp.append(load(wu_ref.at[j], wgu_v.at[:, pl.ds(256 * j + 128, 128)]))
-    wd_cp = [load(wd_ref.at[j], wd_v.at[pl.ds(128 * j, 128)]) for j in range(2)]
-
-    barrier = pltpu.get_barrier_semaphore()
-    peers = [at_p(k) for k in range(1, N_P)]
-    peers += [at_z(k) for k in range(1, N_Z) if k != NZL]
-    peers += [at_x(k) for k in range(1, NX)]
-    peers += [sibling]
-    for peer in peers:
-        pl.semaphore_signal(barrier, inc=1, device_id=peer, device_id_type=MESH)
-
     sent = []
 
     def send(src, dst, peer):
@@ -190,7 +196,7 @@
         coef = jnp.zeros((REQS, 128), F32)
         for k in range(TOPK):
             coef = coef + jnp.where(lane == ids[:, k : k + 1], vals[:, k : k + 1], 0.0)
-        rt[core, x, zlo, pl.ds(REQS * s, REQS), :] = coef
+        rt[core, x, SLOT[0], pl.ds(REQS * s, REQS), :] = coef
 
     for s in range(2):
         q_s[pl.ds(REQS * s, REQS), :] = q_v[s].astype(F32)
@@ -202,6 +208,12 @@
     len_cp.wait()
     for cp in cache_cp:
         cp.wait()
+    ow_cp = load(ow_ref, ow_v)
+    w_cp = []
+    for j in range(2):
+        w_cp.append(load(wg_ref.at[j], wgu_v.at[:, pl.ds(256 * j, 128)]))
+        w_cp.append(load(wu_ref.at[j], wgu_v.at[:, pl.ds(256 * j + 128, 128)]))
+    wd_cp = [load(wd_ref.at[j], wd_v.at[pl.ds(128 * j, 128)]) for j in range(2)]
     for m in range(8):
         picked_v[m] = cache_v[mig_s[0, m], mig_s[1, m]]
 
@@ -259,7 +271,8 @@
     for k in FAR_P:
         a_cp.append(send(a_send.at[lax.rem(p + k, N_P)], a_recv.at[k], at_p(k)))
     rt_cp = [
-        send(rt.at[core, x, zlo], rt.at[core, x, zlo], at_zlo(k)) for k in range(1, NZL)
+        send(rt.at[core, x, SLOT[0]], rt.at[core, x, SLOT[k]], at_zlo(k))
+        for k in range(1, NZL)
     ]
     guest_cp = send(picked_v, guest_ref, at_x(2))
     a_recv[0] = a_send[p]
@@ -343,44 +356,47 @@
     for k, cp in zip((2, 1, 3), b_cp):
         cp.wait_recv()
         hidden = hidden + b_recv[k].astype(F32)
-    zr[z] = hidden.astype(BF16)
-
-    z_cp = [send(zr.at[z], zr.at[z], at_z(k)) for k in FAR_Z]
+    zr[0] = hidden.astype(BF16)
+
+    z_cp = {k: send(zr.at[0], zr.at[k], at_z(k)) for k in Z_LABELS}
     for cp in rt_cp:
         cp.wait_recv()
     rt_cp = [send(rt.at[core], rt.at[core], sibling)]
-    for cp in z_cp:
-        cp.wait_recv()
-    for t in range(NZL):
-        hidden = zr[t].astype(F32) + zr[NZL + t].astype(F32)
-        g_buf[core, ia, ib, t] = hidden.astype(BF16)
-    hidden = zr[zlo].astype(F32) + zr[NZL + zlo].astype(F32)
+    b_cp, a_cp = [], []
+
+    def to_ring(hh, jb):
+        piece = g_buf.at[hh, core, ia, jb]
+        return [send(piece, piece, at_a(k)) for k in (2, 1, 3)]
+
+    for hh in range(2):
+        for n, o in enumerate(OFFSETS[hh]):
+            if o != 0:
+                z_cp[o].wait_recv()
+            z_cp[(o + 4) % 8].wait_recv()
+            hidden = zr[o].astype(F32) + zr[(o + 4) % 8].astype(F32)
+            g_buf[hh, core, ia, ib, n] = hidden.astype(BF16)
+        mine = g_buf.at[hh, core, ia, ib]
+        b_cp.append({k: send(mine, mine, at_b(k)) for k in (2, 1, 3)})
     hid[0] = hidden[0:TOK]
     hid[1] = hidden[TOK : 2 * TOK]
-
-    def to_ring(jb):
-        piece = g_buf.at[core, ia, jb]
-        return [send(piece, piece, at_a(k)) for k in (2, 1, 3)]
-
-    mine = g_buf.at[core, ia, ib]
-    b_cp = {k: send(mine, mine, at_b(k)) for k in (2, 1, 3)}
-    a_cp = [to_ring(ib)]
-    for k in (1, 3, 2):
-        b_cp[k].wait_recv()
-        a_cp.append(to_ring(lax.rem(ib + 4 - k, 4)))
-
+    for hh in range(2):
+        a_cp.append([to_ring(hh, ib)])
     gain_cp.wait()
     ssq[...] = jnp.zeros_like(ssq)
-
-    def prepare(plane, jb):
+    for hh in range(2):
+        for k in (1, 3, 2):
+            b_cp[hh][k].wait_recv()
+            a_cp[hh].append(to_ring(hh, lax.rem(ib + 4 - k, 4)))
+
+    def prepare(hh, plane, jb):
         def step(ja, _):
             xx = (1 - plane) * ja + plane * jb
             yy = plane * ja + (1 - plane) * jb
-            blocks = g_buf[plane, ja, jb].astype(F32)
+            blocks = g_buf[hh, plane, ja, jb].astype(F32)
             rows = jnp.concatenate(
                 [
-                    blocks[:, 0:TOK].reshape(NZL * TOK, PART),
-                    blocks[:, TOK : 2 * TOK].reshape(NZL * TOK, PART),
+                    blocks[:, 0:TOK].reshape(2 * TOK, PART),
+                    blocks[:, TOK : 2 * TOK].reshape(2 * TOK, PART),
                 ],
                 axis=1,
             )
@@ -388,7 +404,9 @@
             while sq.shape[1] > 128:
                 half = sq.shape[1] // 2
                 sq = sq[:, 0:half] + sq[:, half:]
-            at_row = pl.ds(pl.multiple_of(plane * (ALL // 2) + xx * (NZL * TOK), NZL * TOK), NZL * TOK)
+            at_row = pl.ds(
+                pl.multiple_of((hh * 2 + plane) * (ALL // 4) + xx * (2 * TOK), 2 * TOK), 2 * TOK
+            )
             at_col = pl.ds(pl.multiple_of(yy * PAIR, PAIR), PAIR)
             ssq[at_row, :] += sq
             rows_v[at_row, at_col] = (rows * gain_v[:, at_col]).astype(BF16)
@@ -396,116 +414,125 @@
 
         lax.fori_loop(0, 4, step, 0)
 
-    def across(ja, jb):
-        piece = g_buf.at[core, ja, jb]
-        return send(piece, piece, sibling)
-
-    order = (0, 1, 3, 2)
-    c_cp = [[across(ia, lax.rem(ib + 4 - k, 4))] for k in order]
-    for i, k in enumerate(order):
-        jb = lax.rem(ib + 4 - k, 4)
-        for ka, cp in zip((2, 1, 3), a_cp[i]):
+    def receive(hh):
+        order = (0, 1, 3, 2)
+
+        def across(ja, jb):
+            piece = g_buf.at[hh, core, ja, jb]
+            return send(piece, piece, sibling)
+
+        c_cp = [[across(ia, lax.rem(ib + 4 - k, 4))] for k in order]
+        for i, k in enumerate(order):
+            jb = lax.rem(ib + 4 - k, 4)
+            for ka, cp in zip((2, 1, 3), a_cp[hh][i]):
+                cp.wait_recv()
+                c_cp[i].append(across(lax.rem(ia + 4 - ka, 4), jb))
+            prepare(hh, core, jb)
+            if i > 0:
+                for cp in c_cp[i - 1]:
+                    cp.wait_recv()
+                prepare(hh, 1 - core, lax.rem(sib_ib + 4 - order[i - 1], 4))
+        for cp in c_cp[3]:
             cp.wait_recv()
-            c_cp[i].append(across(lax.rem(ia + 4 - ka, 4), jb))
-        prepare(core, jb)
-        if i > 0:
-            for cp in c_cp[i - 1]:
-                cp.wait_recv()
-            prepare(1 - core, lax.rem(sib_ib + 4 - order[i - 1], 4))
-    for cp in c_cp[3]:
-        cp.wait_recv()
-    prepare(1 - core, lax.rem(sib_ib + 4 - order[3], 4))
+        prepare(hh, 1 - core, lax.rem(sib_ib + 4 - order[3], 4))
+
+    def experts(hh):
+        here = slice(hh * (ALL // 2), (hh + 1) * (ALL // 2))
+        spread = jnp.sum(ssq[here, :], -1, keepdims=True) * (1.0 / D)
+        norm = lax.rsqrt(spread + 1e-06)
+        coefs = rt[:, :, 2 * hh : 2 * hh + 2].reshape(ALL // 2, 128)
+        lane = lax.broadcasted_iota(jnp.int32, (ALL // 2, 128), 1)
+        for j in range(2):
+            coef = jnp.sum(jnp.where(lane == 2 * me + j, coefs, 0.0), -1, keepdims=True)
+            both = jnp.dot(
+                rows_v[here, :], wgu_v[:, 256 * j : 256 * j + 256], preferred_element_type=F32
+            )
+            gate = both[:, 0:128] * norm
+            up = both[:, 128:256] * norm
+            inner = gate / (1.0 + jnp.exp(-gate)) * up
+            act[here, 128 * j : 128 * j + 128] = (inner * coef).astype(BF16)
+
+        def down_step(yy, _):
+            at = pl.ds(pl.multiple_of(yy * PAIR, PAIR), PAIR)
+            made = jnp.dot(act[here, :], wd_v[:, at], preferred_element_type=F32)
+            made = made.reshape(2, NX * 2, TOK, PAIR)
+            made = jnp.concatenate([made[..., 0:PART], made[..., PART:PAIR]], axis=2)
+            made = made.astype(BF16).reshape(2, NX, 2, 2 * TOK, PART)
+            p_buf[hh, 0, :, yy] = made[0]
+            p_buf[hh, 1, yy] = made[1]
+            return 0
+
+        lax.fori_loop(0, NY, down_step, 0)
+
+    order = (2, 1, 3, 0)
+
+    def core_sends(hh):
+        cps = []
+        for kb in order:
+            for ka in order:
+                piece = (lax.rem(sib_ia + ka, 4), lax.rem(sib_ib + kb, 4))
+                cps.append(send(p_buf.at[hh, 1 - core, *piece], s_buf.at[hh, *piece], sibling))
+        return cps
+
+    def ring_sends(hh, c_cp):
+        cps = []
+        for i, kb in enumerate(order):
+            jb = lax.rem(ib + kb, 4)
+            for n, ka in enumerate(order):
+                ja = lax.rem(ia + ka, 4)
+                c_cp[4 * i + n].wait_recv()
+                both = p_buf[hh, core, ja, jb].astype(F32) + s_buf[hh, ja, jb].astype(F32)
+                if ka != 0:
+                    m_buf[hh, ja, jb] = both.astype(BF16)
+                    cps.append(send(m_buf.at[hh, ja, jb], a_in.at[hh, i, ka], at_a(ka)))
+                else:
+                    n_buf[hh, i] = both
+        return cps
+
+    e_cp = []
+
+    def last_sends(hh, ring_cp):
+        for i, kb in enumerate(order):
+            total = n_buf[hh, i]
+            for n in range(3):
+                ring_cp[3 * i + n].wait_recv()
+                total = total + a_in[hh, i, order[n]].astype(F32)
+            for n, o in enumerate(OFFSETS[hh]):
+                t_buf[hh, i, n, 0] = total[n, 0:TOK]
+                t_buf[hh, i, n, 1] = total[n, TOK : 2 * TOK]
+                for kz in ((8 - o) % 8, 4 - o):
+                    zz = lax.div(lax.rem(z + kz, N_Z), NZL)
+                    if kb != 0 or kz != 0:
+                        e_send[i, kz] = packed(t_buf[hh, i, n, zz]).astype(BF16)
+                        cp = send(e_send.at[i, kz], e_recv.at[i, kz], at_bz(kb, kz))
+                        e_cp.append((i, kz, cp))
+
+    for cp in w_cp:
+        cp.wait()
+    for cp in wd_cp:
+        cp.wait()
+    receive(0)
     for cp in rt_cp:
         cp.wait_recv()
-
-    for cp in w_cp:
-        cp.wait()
-    spread = jnp.sum(ssq[...], -1, keepdims=True) * (1.0 / D)
-    norm = lax.rsqrt(spread + 1e-06)
-    coefs = rt[...].reshape(ALL, 128)
-    lane = lax.broadcasted_iota(jnp.int32, (ALL, 128), 1)
-    for j in range(2):
-        coef = jnp.sum(jnp.where(lane == 2 * me + j, coefs, 0.0), -1, keepdims=True)
-        both = jnp.dot(
-            rows_v[...], wgu_v[:, 256 * j : 256 * j + 256], preferred_element_type=F32
-        )
-        gate = both[:, 0:128] * norm
-        up = both[:, 128:256] * norm
-        inner = gate / (1.0 + jnp.exp(-gate)) * up
-        act[:, 128 * j : 128 * j + 128] = (inner * coef).astype(BF16)
-
-    for cp in wd_cp:
-        cp.wait()
-
-    def down_step(yy, _):
-        at = pl.ds(pl.multiple_of(yy * PAIR, PAIR), PAIR)
-        made = jnp.dot(act[...], wd_v[:, at], preferred_element_type=F32)
-        made = made.reshape(2, NX * NZL, TOK, PAIR)
-        made = jnp.concatenate([made[..., 0:PART], made[..., PART:PAIR]], axis=2)
-        made = made.astype(BF16).reshape(2, NX, NZL, 2 * TOK, PART)
-        p_buf[0, :, yy] = made[0]
-        p_buf[1, yy] = made[1]
-        return 0
-
-    lax.fori_loop(0, NY, down_step, 0)
-
-    order = (2, 1, 3, 0)
-    c_cp = []
-    for k in order:
-        jb = lax.rem(sib_ib + k, 4)
-        c_cp.append(send(p_buf.at[1 - core, :, jb], s_buf.at[:, jb], sibling))
-    a_cp = []
-    for i, k in enumerate(order):
-        c_cp[i].wait_recv()
-        jb = lax.rem(ib + k, 4)
-        m_buf[:, jb] = (p_buf[core, :, jb].astype(F32) + s_buf[:, jb].astype(F32)).astype(BF16)
-        a_cp.append(
-            [
-                send(m_buf.at[lax.rem(ia + ka, 4), jb], a_in.at[i, ka], at_a(ka))
-                for ka in (2, 1, 3)
-            ]
-        )
-    b_cp = []
-    for i, k in enumerate(order):
-        for cp in a_cp[i]:
-            cp.wait_recv()
-        jb = lax.rem(ib + k, 4)
-        total = m_buf[ia, jb].astype(F32)
-        for ka in range(1, 4):
-            total = total + a_in[i, ka].astype(F32)
-        if k != 0:
-            n_buf[k] = total.astype(BF16)
-            b_cp.append(send(n_buf.at[k], b_in.at[k], at_b(k)))
-    for k, cp in zip(order, b_cp):
+    experts(0)
+    c_0 = core_sends(0)
+    receive(1)
+    a_0 = ring_sends(0, c_0)
+    experts(1)
+    c_1 = core_sends(1)
+    a_1 = ring_sends(1, c_1)
+    last_sends(0, a_0)
+    last_sends(1, a_1)
+    result = packed(hid[zhi]) + packed(t_buf[1, 3, 1, zhi])
+    for i, kz, cp in e_cp:
         cp.wait_recv()
-        total = total + b_in[k].astype(F32)
-    for t in range(NZL):
-        n2_buf[t] = packed(total[t, 0:TOK])
-        n2_buf[NZL + t] = packed(total[t, TOK : 2 * TOK])
-    z_send[...] = n2_buf[...].astype(BF16)
-    z_cp = [send(z_send.at[lax.rem(z + k, N_Z)], z_recv.at[k], at_z(k)) for k in FAR_Z]
-    result = packed(hid[zhi]) + n2_buf[z]
-    for k, cp in zip(FAR_Z, z_cp):
-        cp.wait_recv()
-        result = result + z_recv[k].astype(F32)
+        result = result + e_recv[i, kz].astype(F32)
     o_s[...] = unpacked(result)
     for s in range(2):
         out_ref[s] = o_s[REQS * s : REQS * (s + 1), :].astype(BF16)
     guest_cp.wait_recv()
     for cp in sent:
         cp.wait_send()
-
-
-def finish_kernel(a_ref, b_ref, a_out, b_out, a_v, b_v, sem):
-    pairs = [(a_ref, a_v), (b_ref, b_v), (a_v, a_out), (b_v, b_out)]
-    copies = [pltpu.make_async_copy(*pair, sem.at[i]) for i, pair in enumerate(pairs)]
-    copies[0].start()
-    copies[1].start()
-    for i in range(2):
-        copies[i].wait()
-        copies[i + 2].start()
-    for i in range(2):
-        copies[i + 2].wait()
 
 
 def shards(
@@ -535,11 +562,11 @@
         jax.ShapeDtypeStruct((2, REQS, PART), BF16),
         jax.ShapeDtypeStruct((8, ROWS, 512), BF16),
     )
-    made = pl.pallas_call(
+    return pl.pallas_call(
         kernel,
-        out_shape=shapes,
+        out_shape=tuple(pltpu.VMEM(v.shape, v.dtype) for v in shapes),
         in_specs=[hbm] * 13,
-        out_specs=(vmem, hbm),
+        out_specs=(vmem, vmem),
         scratch_shapes=[
             buf(2, REQS, D),
             buf(2, REQS, 512),
@@ -565,19 +592,18 @@
             buf(N_Z, *pair),
             buf(2, TOK, PART, dtype=F32),
             buf(2, NX, NZL, TOK, 128, dtype=F32),
-            buf(2, 4, 4, NZL, *pair),
+            buf(2, 2, 4, 4, 2, *pair),
             buf(ALL, D),
             buf(ALL, 128, dtype=F32),
             buf(ALL, 256),
-            buf(2, 4, 4, NZL, *pair),
-            buf(4, 4, NZL, *pair),
-            buf(4, 4, NZL, *pair),
-            buf(4, 4, NZL, *pair),
-            buf(4, NZL, *pair),
-            buf(4, NZL, *pair),
-            buf(N_Z, *block, dtype=F32),
-            buf(N_Z, *block),
-            buf(N_Z, *block),
+            buf(2, 2, 4, 4, 2, *pair),
+            buf(2, 4, 4, 2, *pair),
+            buf(2, 4, 4, 2, *pair),
+            buf(2, 4, 4, 2, *pair),
+            buf(2, 4, 2, *pair, dtype=F32),
+            buf(2, 4, 2, 2, TOK, PART, dtype=F32),
+            buf(4, N_Z, *block),
+            buf(4, N_Z, *block),
             buf(TOK, PART, dtype=F32),
             pltpu.SemaphoreType.DMA((24,)),
             pltpu.SemaphoreType.DMA((N_SEMS,)),
@@ -604,18 +630,6 @@
         w_up,
         w_down,
     )
-    return pl.pallas_call(
-        finish_kernel,
-        out_shape=shapes,
-        in_specs=[hbm] * 2,
-        out_specs=(hbm, hbm),
-        scratch_shapes=[
-            buf(2, REQS, PART),
-            buf(8, ROWS, 512),
-            pltpu.SemaphoreType.DMA((4,)),
-        ],
-        compiler_params=pltpu.CompilerParams(vmem_limit_bytes=60 * MIB),
-    )(*made)
 
 
 def solution(mesh):

time: 64.5 us -> 61 us (0.946)
  Pallas kernels: 63.3 us -> 58.4 us
  local copies, waits for them, and re-layouts: 0 us -> 1.26 us
    pallas_call x2 -> x1, Pallas kernels: 63.3 us -> 58.4 us  [shards(): pl.pallas_call(kernel, out_shape=tuple((pltpu.VMEM(v.shape, v.dtype) for...]
    unnamed x0 -> x2, local copies, waits for them, and re-layouts: none -> 1.26 us
where the time goes in v4:
time: 61 us; the launch traced here: 60.3 us
  Pallas kernels  58.4 us (96%)
  local copies, waits for them, and re-layouts  1.26 us (2%)
  between operations  0.64 us (1%)
    pallas_call x1, Pallas kernels, shards(): pl.pallas_call(kernel, out_shape=tuple((pltpu.VMEM(v.shape, v.dtype) for...  58.4 us
    unnamed x2, local copies, waits for them, and re-layouts  1.26 us

profile of v4, /device:TPU:2, one launch (start us, length us, event | category | flops | bytes accessed | tf_op | source)
XLA Modules:
  0.0 60.3 jit_solution(553960405826872434)
XLA Ops:
  0.6 58.4 %shard_map.140 = (bf16[2,4,512]{2,1,0:T(4,128)(2,1)S(1)}, bf16[8,16,512]{2,1,0:T(8,128)(2,1)S(1)}) custom-call(bf16[2,4,4096]{2,1,0:T(4,128)(2,1)} %q_ref.1, bf16[2,4,512]{2,1,0:T(4,128)(2,1)} %fresh_ref.1, bf16[4,32,16,512]{3,2,1,0:T(8,128)(2,1)} %cache_ref.1, s32[1,4]{1,0:T(1,128)} %bitcast.5, s32[2,8]{1,0:T(2,128)} %bitcast.4, ...), custom_call_target="tpu_custom_call" | custom-call | flops 2000000000 | bytes 13631488 | tf_op jit(solution)/shard_map/pallas_call | solution.py:565
  59.1 0.6 copy.17
  59.7 0.7 %copy.18 = bf16[8,16,512]{2,1,0:T(8,128)(2,1)} copy(bf16[8,16,512]{2,1,0:T(8,128)(2,1)S(1)} %get-tuple-element.3) | data formatting | bytes 262144

commit v5 on v4

--- a/solution.py
+++ b/solution.py
@@ -412,7 +412,8 @@
             rows_v[at_row, at_col] = (rows * gain_v[:, at_col]).astype(BF16)
             return 0
 
-        lax.fori_loop(0, 4, step, 0)
+        for ja in range(4):
+            step(ja, 0)
 
     def receive(hh):
         order = (0, 1, 3, 2)
@@ -442,11 +443,10 @@
         norm = lax.rsqrt(spread + 1e-06)
         coefs = rt[:, :, 2 * hh : 2 * hh + 2].reshape(ALL // 2, 128)
         lane = lax.broadcasted_iota(jnp.int32, (ALL // 2, 128), 1)
+        all_up = jnp.dot(rows_v[here, :], wgu_v[...], preferred_element_type=F32)
         for j in range(2):
             coef = jnp.sum(jnp.where(lane == 2 * me + j, coefs, 0.0), -1, keepdims=True)
-            both = jnp.dot(
-                rows_v[here, :], wgu_v[:, 256 * j : 256 * j + 256], preferred_element_type=F32
-            )
+            both = all_up[:, 256 * j : 256 * j + 256]
             gate = both[:, 0:128] * norm
             up = both[:, 128:256] * norm
             inner = gate / (1.0 + jnp.exp(-gate)) * up
@@ -462,7 +462,8 @@
             p_buf[hh, 1, yy] = made[1]
             return 0
 
-        lax.fori_loop(0, NY, down_step, 0)
+        for k in range(NY):
+            down_step(k, 0)
 
     order = (2, 1, 3, 0)
 
@@ -520,9 +521,13 @@
     a_0 = ring_sends(0, c_0)
     experts(1)
     c_1 = core_sends(1)
+    guest_cp.wait_recv()
     a_1 = ring_sends(1, c_1)
     last_sends(0, a_0)
     last_sends(1, a_1)
+    n_last = len(sent) - len(e_cp)
+    for cp in sent[:n_last]:
+        cp.wait_send()
     result = packed(hid[zhi]) + packed(t_buf[1, 3, 1, zhi])
     for i, kz, cp in e_cp:
         cp.wait_recv()
@@ -530,8 +535,7 @@
     o_s[...] = unpacked(result)
     for s in range(2):
         out_ref[s] = o_s[REQS * s : REQS * (s + 1), :].astype(BF16)
-    guest_cp.wait_recv()
-    for cp in sent:
+    for cp in sent[n_last:]:
         cp.wait_send()
 
 

time: 61 us -> 60 us (0.984)
  Pallas kernels: 58.4 us -> 57.3 us
    pallas_call x1, Pallas kernels: 58.4 us -> 57.3 us  [shards(): pl.pallas_call(kernel, out_shape=tuple((pltpu.VMEM(v.shape, v.dtype) for...]
where the time goes in v5:
time: 60 us; the launch traced here: 59.2 us
  Pallas kernels  57.3 us (96%)
  local copies, waits for them, and re-layouts  1.26 us (2%)
  between operations  0.64 us (1%)
    pallas_call x1, Pallas kernels, shards(): pl.pallas_call(kernel, out_shape=tuple((pltpu.VMEM(v.shape, v.dtype) for...  57.3 us
    unnamed x2, local copies, waits for them, and re-layouts  1.26 us

profile of v5, /device:TPU:2, one launch (start us, length us, event | category | flops | bytes accessed | tf_op | source)
XLA Modules:
  0.0 59.2 jit_solution(335008802301130093)
XLA Ops:
  0.6 57.3 %shard_map.140 = (bf16[2,4,512]{2,1,0:T(4,128)(2,1)S(1)}, bf16[8,16,512]{2,1,0:T(8,128)(2,1)S(1)}) custom-call(bf16[2,4,4096]{2,1,0:T(4,128)(2,1)} %q_ref.1, bf16[2,4,512]{2,1,0:T(4,128)(2,1)} %fresh_ref.1, bf16[4,32,16,512]{3,2,1,0:T(8,128)(2,1)} %cache_ref.1, s32[1,4]{1,0:T(1,128)} %bitcast.5, s32[2,8]{1,0:T(2,128)} %bitcast.4, ...), custom_call_target="tpu_custom_call" | custom-call | flops 2000000000 | bytes 13631488 | tf_op jit(solution)/shard_map/pallas_call | solution.py:569
  58.0 0.6 %copy.17 = bf16[2,4,512]{2,1,0:T(4,128)(2,1)} copy(bf16[2,4,512]{2,1,0:T(4,128)(2,1)S(1)} %get-tuple-element.2) | data formatting | bytes 16384
  58.6 0.7 %copy.18 = bf16[8,16,512]{2,1,0:T(8,128)(2,1)} copy(bf16[8,16,512]{2,1,0:T(8,128)(2,1)S(1)} %get-tuple-element.3) | data formatting | bytes 262144

commit v6 on v5

--- a/solution.py
+++ b/solution.py
@@ -415,27 +415,32 @@
         for ja in range(4):
             step(ja, 0)
 
-    def receive(hh):
+    from_core = [[], []]
+
+    def absorb(hh, i):
+        for cp in from_core[hh][i]:
+            cp.wait_recv()
+        prepare(hh, 1 - core, lax.rem(sib_ib + 4 - (0, 1, 3, 2)[i], 4))
+
+    def receive(hh, first, last):
         order = (0, 1, 3, 2)
 
         def across(ja, jb):
             piece = g_buf.at[hh, core, ja, jb]
             return send(piece, piece, sibling)
 
-        c_cp = [[across(ia, lax.rem(ib + 4 - k, 4))] for k in order]
-        for i, k in enumerate(order):
-            jb = lax.rem(ib + 4 - k, 4)
+        for i in range(first, last):
+            jb = lax.rem(ib + 4 - order[i], 4)
+            cps = [across(ia, jb)]
             for ka, cp in zip((2, 1, 3), a_cp[hh][i]):
                 cp.wait_recv()
-                c_cp[i].append(across(lax.rem(ia + 4 - ka, 4), jb))
+                cps.append(across(lax.rem(ia + 4 - ka, 4), jb))
+            from_core[hh].append(cps)
             prepare(hh, core, jb)
             if i > 0:
-                for cp in c_cp[i - 1]:
-                    cp.wait_recv()
-                prepare(hh, 1 - core, lax.rem(sib_ib + 4 - order[i - 1], 4))
-        for cp in c_cp[3]:
-            cp.wait_recv()
-        prepare(hh, 1 - core, lax.rem(sib_ib + 4 - order[3], 4))
+                absorb(hh, i - 1)
+        if last == 4:
+            absorb(hh, 3)
 
     def experts(hh):
         here = slice(hh * (ALL // 2), (hh + 1) * (ALL // 2))
@@ -512,12 +517,13 @@
         cp.wait()
     for cp in wd_cp:
         cp.wait()
-    receive(0)
+    receive(0, 0, 4)
+    receive(1, 0, 1)
     for cp in rt_cp:
         cp.wait_recv()
     experts(0)
     c_0 = core_sends(0)
-    receive(1)
+    receive(1, 1, 4)
     a_0 = ring_sends(0, c_0)
     experts(1)
     c_1 = core_sends(1)

time: 60 us -> 59.8 us (level)
  no operation moved by 1% of the time
where the time goes in v6:
time: 59.8 us; the launch traced here: 59.1 us
  Pallas kernels  57.2 us (96%)
  local copies, waits for them, and re-layouts  1.26 us (2%)
  between operations  0.64 us (1%)
    pallas_call x1, Pallas kernels, shards(): pl.pallas_call(kernel, out_shape=tuple((pltpu.VMEM(v.shape, v.dtype) for...  57.2 us
    unnamed x2, local copies, waits for them, and re-layouts  1.26 us

profile of v6, /device:TPU:2, one launch (start us, length us, event | category | flops | bytes accessed | tf_op | source)
XLA Modules:
  0.0 59.1 jit_solution(4345753902405496416)
XLA Ops:
  0.6 57.2 %shard_map.140 = (bf16[2,4,512]{2,1,0:T(4,128)(2,1)S(1)}, bf16[8,16,512]{2,1,0:T(8,128)(2,1)S(1)}) custom-call(bf16[2,4,4096]{2,1,0:T(4,128)(2,1)} %q_ref.1, bf16[2,4,512]{2,1,0:T(4,128)(2,1)} %fresh_ref.1, bf16[4,32,16,512]{3,2,1,0:T(8,128)(2,1)} %cache_ref.1, s32[1,4]{1,0:T(1,128)} %bitcast.5, s32[2,8]{1,0:T(2,128)} %bitcast.4, ...), custom_call_target="tpu_custom_call" | custom-call | flops 2000000000 | bytes 13631488 | tf_op jit(solution)/shard_map/pallas_call | solution.py:575
  57.9 0.6 %copy.17 = bf16[2,4,512]{2,1,0:T(4,128)(2,1)} copy(bf16[2,4,512]{2,1,0:T(4,128)(2,1)S(1)} %get-tuple-element.2) | data formatting | bytes 16384
  58.5 0.7 %copy.18 = bf16[8,16,512]{2,1,0:T(8,128)(2,1)} copy(bf16[8,16,512]{2,1,0:T(8,128)(2,1)S(1)} %get-tuple-element.3) | data formatting | bytes 262144
